TPU v7x, 256 devices: a whole 4x4x8 slice. The times are simulated.
256 devices in a mesh: vocab: 16 (over x, y), dp: 16 (over z, core).
Axes of the slice: x: 4, y: 4, z: 8, core: 2. Of those that a mesh axis runs over, the one named last changes fastest.
Arguments:
- hidden: bfloat16 [512, 5120], P('dp')
- table: bfloat16 [131072, 5120], P(('vocab', 'dp'))
- embed_grad: bfloat16 [512, 5120], P('dp'), may hold values from -1.1953125 to 1.1953125
- token_ids: int32 [512], P('dp'), may hold values from 0 to 131071
- target_ids: int32 [512], P('dp'), may hold values from 0 to 131071
Outputs:
- grad_hidden: bfloat16 [512, 5120], P('dp', 'vocab')
- grad_table: bfloat16 [131072, 5120], P(('vocab', 'dp'))
- loss_sum: float32 [], replicated
All inputs are finite; a program needn't handle non-finite values.
Results may differ from a plain program's by a relative error of at most 0.0037.
Values may be sent and summed in bfloat16 or wider, within the bound.
No kernel may reach another device: no remote copies, remote signals or barrier semaphores. Data moves between devices by JAX's collectives and lax.ppermute only.
A program may use at most 128 MiB of HBM per device.

v0:
```python
import jax
import jax.numpy as jnp
from jax import lax
from jax.sharding import PartitionSpec as P


def per_device(hidden, table, embed_grad, token_ids, target_ids):
    rows_all, targets_all = (
        lax.all_gather(hidden, "dp", axis=0, tiled=True),
        lax.all_gather(target_ids, "dp", axis=0, tiled=True),
    )
    row_count = table.shape[0]
    dp_count = lax.axis_size("dp")
    offset_row = (lax.axis_index("vocab") * dp_count + lax.axis_index("dp")) * row_count
    logits = lax.dot_general(
        rows_all, table, (((1,), (1,)), ((), ())), preferred_element_type=jnp.float32
    )
    columns = offset_row + jnp.arange(row_count, dtype=jnp.int32)
    target_hit = targets_all[:, None] == columns[None, :]
    local_target = jnp.sum(jnp.where(target_hit, logits, jnp.float32(0.0)), axis=1)
    local_top = jnp.max(logits, axis=1)
    row_top = lax.pmax(local_top, ("vocab", "dp"))
    shifted = jnp.exp(logits - row_top[:, None])
    row_total, target_logit = lax.psum((jnp.sum(shifted, axis=1), local_target), ("vocab", "dp"))
    loss_sum = jnp.sum(row_top + jnp.log(row_total) - target_logit)
    dlogits = (shifted / row_total[:, None] - target_hit.astype(jnp.float32)).astype(jnp.bfloat16)
    head_grad = lax.dot_general(
        dlogits, rows_all, (((0,), (0,)), ((), ())), preferred_element_type=jnp.float32
    )
    grads_all, tokens_all = (
        lax.all_gather(embed_grad, "dp", axis=0, tiled=True),
        lax.all_gather(token_ids, "dp", axis=0, tiled=True),
    )
    onehot_tok = (tokens_all[:, None] == columns[None, :]).astype(jnp.bfloat16)
    embed_term = lax.dot_general(
        onehot_tok, grads_all, (((0,), (0,)), ((), ())), preferred_element_type=jnp.float32
    )
    grad_table = (head_grad + embed_term).astype(jnp.bfloat16)
    token_part = lax.psum_scatter(
        jnp.dot(dlogits, table, preferred_element_type=jnp.float32),
        "dp",
        scatter_dimension=0,
        tiled=True,
    )
    grad_hidden = lax.psum_scatter(token_part, "vocab", scatter_dimension=1, tiled=True).astype(
        jnp.bfloat16
    )
    return (grad_hidden, grad_table, loss_sum)


def solution(mesh):
    in_specs = (P("dp", None), P(("vocab", "dp"), None), P("dp", None), P("dp"), P("dp"))
    out_specs = (P("dp", "vocab"), P(("vocab", "dp"), None), P())
    return jax.shard_map(
        per_device, mesh=mesh, in_specs=in_specs, out_specs=out_specs, check_vma=False
    )
```

profile of v0, /device:TPU:8, one launch (start us, length us, event | category | flops | bytes accessed | tf_op | source)
XLA Modules:
  0.0 426.3 jit_solution(7708347716300214621)
XLA Ops:
  7.2 0.0 all-gather.3.cloned.1.call-start
  7.2 0.7 all-gather.3.cloned.1.call-update
  7.9 0.0 reduce-scatter.5.cloned.1.call-start
  8.0 1.3 dynamic-slice
  9.9 0.9 dynamic-update-slice
  10.7 0.8 dynamic-update-slice.1
  11.6 16.4 %all-reduce.2 = (s32[512]{0:T(512)S(1)}, s32[512]{0:T(512)S(1)}) all-reduce(s32[512]{0:T(512)S(1)} %dynamic-update-slice, s32[512]{0:T(512)S(1)} %dynamic-update-slice.1), channel_id=1, replica_groups=mesh['vocab'=16,'dp'=16] {'dp'}, use_global_device_ids=true, to_apply=%add | all-reduce | flops 1024 | bytes 8192
  28.0 28.1 %all-gather.3.cloned.1.call-done = bf16[512,5120]{1,0:T(8,128)(2,1)} async-done(((bf16[32,5120]{1,0:T(8,128)(2,1)}), bf16[512,5120]{1,0:T(8,128)(2,1)}) %all-gather.3.cloned.1.call-update) | async-done | bytes 5242896 | tf_op jit(solution)/shard_map/all_gather | solution.py:9
  56.1 6.4 %fusion.11 = (f32[512]{0:T(512)S(1)}, f32[512,512]{0,1:T(8,128)S(1)}) fusion(bf16[512,5120]{1,0:T(8,128)(2,1)} %all-gather.3.cloned.1.call-done, bf16[512,5120]{1,0:T(8,128)(2,1)} %param.6), kind=kOutput, calls=%fused_computation.15 | convolution fusion | flops 2684616192 | bytes 11536384 | tf_op jit(solution)/shard_map/dot_general | solution.py:15
  62.5 75.2 %pmax.7 = f32[512]{0:T(512)S(1)} all-reduce(f32[512]{0:T(512)S(1)} %get-tuple-element.9), channel_id=1, replica_groups=mesh['vocab'=16,'dp'=16] {'vocab','dp'}, use_global_device_ids=true, to_apply=%region_1.2 | all-reduce | flops 512 | bytes 4096 | tf_op jit(solution)/shard_map/pmax | solution.py:22
  137.7 0.3 fusion.2
  137.9 73.4 %all-reduce.3 = (f32[512]{0:T(512)S(1)}, f32[512]{0:T(512)S(1)}) all-reduce(f32[512]{0:T(512)S(1)} %get-tuple-element.4, f32[512]{0:T(512)S(1)} %get-tuple-element.3), channel_id=1, replica_groups=mesh['vocab'=16,'dp'=16] {'vocab','dp'}, use_global_device_ids=true, to_apply=%region_3.4 | all-reduce | flops 1024 | bytes 8192 | tf_op jit(solution)/shard_map/psum | solution.py:24
  211.3 8.2 %fusion.9 = f32[512,5120]{1,0:T(8,128)} fusion(bf16[512,5120]{1,0:T(8,128)(2,1)} %param.6, f32[512,512]{0,1:T(8,128)S(1)} %get-tuple-element.10, s32[512]{0:T(512)S(1)} %get-tuple-element.5, f32[512]{0:T(512)S(1)} %get-tuple-element.7, f32[512]{0:T(512)S(1)} %pmax.7, s32[512]{0:T(512)S(1)} %iota_add_fusion), kind=kOutput, calls=%fused_computation.14 | convolution fusion | flops 2685927424 | bytes 16785408 | tf_op jit(solution)/shard_map/dot_general | solution.py:40
  219.5 0.0 all-gather.5.cloned.1.call-start
  219.6 0.7 all-gather.5.cloned.1.call-update
  220.3 0.0 reduce-scatter.7.cloned.1.call-start
  220.3 70.9 %reduce-scatter.5.cloned.1.call-done = f32[32,5120]{1,0:T(8,128)} async-done(((f32[512,5120]{1,0:T(8,128)}), f32[32,5120]{1,0:T(8,128)}) %reduce-scatter.5.cloned.1.call-update) | async-done | bytes 655376 | tf_op jit(solution)/shard_map/reduce_scatter | solution.py:39
  291.2 2.9 copy.8
  294.2 8.2 %fusion.7 = f32[512,5120]{1,0:T(8,128)} fusion(bf16[512,5120]{1,0:T(8,128)(2,1)} %all-gather.3.cloned.1.call-done, f32[512,512]{0,1:T(8,128)S(1)} %get-tuple-element.10, s32[512]{0:T(512)S(1)} %get-tuple-element.5, f32[512]{0:T(512)S(1)} %get-tuple-element.7, f32[512]{0:T(512)S(1)} %pmax.7, s32[512]{0:T(512)S(1)} %iota_add_fusion), kind=kOutput, calls=%fused_computation.13 | convolution fusion | flops 2685927424 | bytes 16785408 | tf_op jit(solution)/shard_map/dot_general | solution.py:27
  302.3 0.6 subtract_reduce_fusion
  303.0 33.2 %all-gather.5.cloned.1.call-done = bf16[512,5120]{1,0:T(8,128)(2,1)} async-done(((bf16[32,5120]{1,0:T(8,128)(2,1)}), bf16[512,5120]{1,0:T(8,128)(2,1)}) %all-gather.5.cloned.1.call-update) | async-done | bytes 5242896 | tf_op jit(solution)/shard_map/all_gather | solution.py:31
  336.2 8.8 %add_convert_fusion = bf16[512,5120]{1,0:T(8,128)(2,1)} fusion(f32[512,5120]{1,0:T(8,128)} %fusion.7, bf16[512,5120]{1,0:T(8,128)(2,1)} %all-gather.5.cloned.1.call-done, s32[512]{0:T(512)S(1)} %get-tuple-element.6, s32[512]{0:T(512)S(1)} %iota_add_fusion), kind=kOutput, calls=%fused_computation | convolution fusion | flops 2689859584 | bytes 20975616 | tf_op jit(solution)/shard_map/dot_general | solution.py:35
  345.0 73.2 %reduce-scatter.7.cloned.1.call-done = f32[320,32]{1,0:T(8,128)} async-done(((f32[5120,32]{1,0:T(8,128)}), f32[320,32]{1,0:T(8,128)}) %reduce-scatter.7.cloned.1.call-update) | async-done | bytes 40976
  418.2 1.6 copy.9
  (5 shorter events, 0.0 us)
Async XLA Ops:
  7.2 48.9 %all-gather.3.cloned.1.call-start = ((), (), s32[]{:S(2)}) async-start(), calls=%async_computation.2 | async-start | bytes 5570560 | tf_op jit(solution)/shard_map/all_gather | solution.py:9
  7.9 283.3 %reduce-scatter.5.cloned.1.call-start = ((), (), s32[]{:S(2)}) async-start(), calls=%async_computation.3 | async-start | bytes 11141120 | tf_op jit(solution)/shard_map/reduce_scatter | solution.py:39
  219.5 116.6 %all-gather.5.cloned.1.call-start = ((), (), s32[]{:S(2)}) async-start(), calls=%async_computation.4 | async-start | bytes 5570560 | tf_op jit(solution)/shard_map/all_gather | solution.py:31
  220.3 197.9 %reduce-scatter.7.cloned.1.call-start = ((), (), s32[]{:S(2)}) async-start(), calls=%async_computation.5 | async-start | bytes 2785280
Sparse Core Ops, SparseCore 0:
  9.8 46.1 all-gather.2
  219.7 71.5 reduce-scatter.4
  293.1 43.0 all-gather.4
  339.6 78.5 reduce-scatter.6
where the time goes:
time: 427 us; the launch traced here: 426 us
  waiting for transfers between devices  207 us (48%)
  blocking collectives  165 us (39%)
  matrix products  31.6 us (7%)
  between operations  14.4 us (3%)
  local copies, waits for them, and re-layouts  7.48 us (2%)
    pmax x1, blocking collectives, per_device(): row_top = lax.pmax(local_top, ('vocab', 'dp'))  75.2 us
    unnamed x5, waiting for transfers between devices  74.6 us
    psum x1, blocking collectives, per_device(): lax.psum((jnp.sum(shifted, axis=1), local_target), ('vocab', 'dp'))  73.4 us
    reduce_scatter x1, waiting for transfers between devices, per_device(): lax.psum_scatter(jnp.dot(dlogits, table, preferred_element_type=jnp.float...  70.9 us
    all_gather x1, waiting for transfers between devices, per_device(): lax.all_gather(embed_grad, 'dp', axis=0, tiled=True)  33.2 us
    all_gather x1, waiting for transfers between devices, per_device(): lax.all_gather(hidden, 'dp', axis=0, tiled=True)  28.1 us
    unnamed x1, blocking collectives  16.4 us
    dot_general x1, matrix products, per_device(): lax.dot_general(onehot_tok, grads_all, (((0,), (0,)), ((), ())), preferre...  8.81 us
  transfers between devices with their start and end apart: 4, of which 4 were waited for; matrix products, arithmetic and copies ran while one was open for 6% of the time, Pallas kernels for 0%

commit v1 on v0

v1 whole, which is shorter than its diff:
```python
import functools

import jax
import jax.numpy as jnp
from jax import lax
from jax.experimental import pallas as pl
from jax.experimental.pallas import tpu as pltpu
from jax.sharding import Mesh
from jax.sharding import PartitionSpec as P

XY = ("x", "y")
XYZ = ("x", "y", "z")
ALL = ("x", "y", "z", "c")
F32 = jnp.float32
BF16 = jnp.bfloat16
CHUNK = 512
LIMIT = 48 * 1024 * 1024


def _params():
    return pltpu.CompilerParams(vmem_limit_bytes=LIMIT)


def _cost(flops, moved):
    return pl.CostEstimate(flops=flops, bytes_accessed=moved, transcendentals=0)


def _const(*zeros):
    return lambda i: zeros


def _row_ids(pos_ref, rows, tokens):
    at = lax.broadcasted_iota(jnp.int32, (2 * rows, tokens), 0)
    return jnp.where(at < rows, pos_ref[1] + at, pos_ref[2] + at - rows)


def _logits_kernel(steps, rows, pos_ref, tgt_ref, *refs):
    pieces, (own_ref, oth_ref, logit_ref, hid_ref, stat_ref) = refs[:-5], refs[-5:]
    step = pl.program_id(0)
    h = jnp.concatenate([p[...] for p in pieces], axis=0)
    hid_ref[...] = h
    dims = (((1,), (1,)), ((), ()))
    a = lax.dot_general(own_ref[...], h, dims, preferred_element_type=F32)
    b = lax.dot_general(oth_ref[...], h, dims, preferred_element_type=F32)

    @pl.when(step == 0)
    def _():
        logit_ref[:rows] = a
        logit_ref[rows:] = b

    @pl.when(step > 0)
    def _():
        logit_ref[:rows] += a
        logit_ref[rows:] += b

    @pl.when(step == steps - 1)
    def _():
        z = pos_ref[0]
        logit = logit_ref[...]
        tokens = logit.shape[1]
        block = tokens // 8
        tgt = pltpu.roll(jnp.broadcast_to(tgt_ref[...], (8, tokens)), lax.rem(8 - z, 8) * block, 1)[:1]
        top = jnp.max(logit, axis=0, keepdims=True)
        total = jnp.sum(jnp.exp(logit - top), axis=0, keepdims=True)
        hit = _row_ids(pos_ref, rows, tokens) == tgt
        own = jnp.sum(jnp.where(hit, logit, 0.0), axis=0, keepdims=True)
        stack = jnp.concatenate([top, total, own, jnp.zeros((5, tokens), F32)], axis=0)
        stat_ref[...] = pltpu.roll(stack, z * block, 1)


def _grad_hidden_kernel(rows, pos_ref, stat_ref, tgt_ref, logit_ref, own_ref, oth_ref, part_ref, dl_ref, loss_ref, dl_t):
    step = pl.program_id(0)

    @pl.when(step == 0)
    def _():
        z = pos_ref[0]
        tokens = logit_ref.shape[1]
        block = tokens // 8
        back = lax.rem(8 - z, 8) * block
        tops = stat_ref[:, 0:2, :]
        sums = stat_ref[:, 2:4, :]
        top = jnp.max(tops, axis=0)
        total = jnp.sum(sums * jnp.exp(tops - top[None]), axis=0)
        hit_sum = jnp.sum(stat_ref[:, 4:6, :], axis=0)
        loss_ref[...] = jnp.sum(top + jnp.log(total) - hit_sum, keepdims=True)

        def rolled(v):
            flat = jnp.concatenate([v[0:1], v[1:2]], axis=1)
            return pltpu.roll(jnp.broadcast_to(flat, (8, tokens)), back, 1)[:1]

        top_row = rolled(top)
        inv_row = rolled(1.0 / total)
        tgt = pltpu.roll(jnp.broadcast_to(tgt_ref[...], (8, tokens)), back, 1)[:1]
        hit = _row_ids(pos_ref, rows, tokens) == tgt
        dl = jnp.exp(logit_ref[...] - top_row) * inv_row - jnp.where(hit, 1.0, 0.0)
        dl_ref[...] = dl.astype(BF16)
        dl_t[...] = dl.T.astype(BF16)

    part = jnp.dot(dl_t[:, :rows], own_ref[...], preferred_element_type=F32)
    part += jnp.dot(dl_t[:, rows:], oth_ref[...], preferred_element_type=F32)
    part_ref[...] = part.T.astype(BF16)


def _sum_kernel(pos_ref, got_ref, out_ref):
    z = pos_ref[0]
    total = jnp.sum(got_ref[...].astype(F32), axis=0).T
    block = total.shape[0] // 8
    for r in range(8):
        out_ref[lax.rem(z + r, 8)] = total[r * block : (r + 1) * block]


def _grad_table_kernel(pos_ref, tok_ref, dl_own_ref, dl_oth_ref, h_own_ref, h_oth_ref, e_ref, out_ref, hot):
    @pl.when(pl.program_id(0) == 0)
    def _():
        at = lax.broadcasted_iota(jnp.int32, hot.shape, 0) + pos_ref[1]
        hot[...] = jnp.where(at == tok_ref[...], 1.0, 0.0).astype(BF16)

    acc = jnp.dot(dl_own_ref[...], h_own_ref[...], preferred_element_type=F32)
    acc += jnp.dot(dl_oth_ref[...], h_oth_ref[...], preferred_element_type=F32)
    acc += jnp.dot(hot[...], e_ref[...], preferred_element_type=F32)
    out_ref[...] = acc.astype(BF16)


def per_device(hidden, table, embed_grad, token_ids, target_ids):
    rows, width = table.shape
    n_tok = hidden.shape[0]
    nz = lax.axis_size("z")
    tokens = n_tok * nz
    xi, yi, zi, ci = (lax.axis_index(a) for a in ALL)
    base = ((xi * 4 + yi) * nz + zi) * 2
    pos = jnp.stack([zi, (base + ci) * rows, (base + 1 - ci) * rows]).astype(jnp.int32)
    swap = [(0, 1), (1, 0)]
    up = [(i, (i + 1) % nz) for i in range(nz)]
    down = [(i, (i - 1) % nz) for i in range(nz)]

    table_oth = lax.ppermute(table, "c", swap)
    u, d, ups, downs = hidden, hidden, [], []
    for _ in range(3):
        u, d = lax.optimization_barrier((lax.ppermute(u, "z", up), lax.ppermute(d, "z", down)))
        ups.append(u)
        downs.append(d)
    half = n_tok // 2
    far = [lax.ppermute(u[:half], "z", up), lax.ppermute(d[half:], "z", down)]
    pieces = [hidden, *downs, *far, *ups[::-1]]

    ids = jnp.concatenate([target_ids, token_ids])
    ids = lax.all_to_all(jnp.broadcast_to(ids[None], (2 * nz, 2 * n_tok)), ("z", "c"), 0, 0, tiled=True)
    targets = lax.dynamic_index_in_dim(ids.reshape(nz, 2, 2 * n_tok), ci, 1, False)[:, :n_tok].reshape(1, tokens)
    toks = ids[:, n_tok:].reshape(1, 2 * tokens)

    steps = width // CHUNK
    smem = pl.BlockSpec(memory_space=pltpu.SMEM)
    col = lambda n: pl.BlockSpec((n, CHUNK), lambda i: (0, i))
    logit, h_own, stat = pl.pallas_call(
        functools.partial(_logits_kernel, steps, rows),
        grid=(steps,),
        in_specs=[smem, pl.BlockSpec((1, tokens), _const(0, 0)), *[col(p.shape[0]) for p in pieces], col(rows), col(rows)],
        out_specs=[
            pl.BlockSpec((2 * rows, tokens), _const(0, 0)),
            col(tokens),
            pl.BlockSpec((8, tokens), _const(0, 0)),
        ],
        out_shape=[
            jax.ShapeDtypeStruct((2 * rows, tokens), F32),
            jax.ShapeDtypeStruct((tokens, width), BF16),
            jax.ShapeDtypeStruct((8, tokens), F32),
        ],
        compiler_params=_params(),
        cost_estimate=_cost(4 * rows * tokens * width, 4 * rows * width + 4 * tokens * width),
        name="logits",
    )(pos, targets, *pieces, table, table_oth)

    e_src, _ = lax.optimization_barrier((embed_grad, far[0]))
    e_all = lax.all_gather(e_src, ("z", "c"), axis=0, tiled=True)

    lanes = 128
    payload = stat[:4].reshape(8, lanes)
    peers = lax.axis_size(XYZ)
    stats = lax.all_to_all(jnp.broadcast_to(payload[None], (peers, 8, lanes)), XYZ, 0, 0, tiled=True)
    h_src, stats = lax.optimization_barrier((h_own, stats))
    h_oth = lax.ppermute(h_src, "c", swap)

    part, dl, loss = pl.pallas_call(
        functools.partial(_grad_hidden_kernel, rows),
        grid=(steps,),
        in_specs=[
            smem,
            pl.BlockSpec((peers, 8, lanes), _const(0, 0, 0)),
            pl.BlockSpec((1, tokens), _const(0, 0)),
            pl.BlockSpec((2 * rows, tokens), _const(0, 0)),
            col(rows),
            col(rows),
        ],
        out_specs=[
            pl.BlockSpec((CHUNK, tokens), lambda i: (i, 0)),
            pl.BlockSpec((2 * rows, tokens), _const(0, 0)),
            pl.BlockSpec((1, 1), _const(0, 0)),
        ],
        out_shape=[
            jax.ShapeDtypeStruct((width, tokens), BF16),
            jax.ShapeDtypeStruct((2 * rows, tokens), BF16),
            jax.ShapeDtypeStruct((1, 1), F32),
        ],
        scratch_shapes=[pltpu.VMEM((tokens, 2 * rows), BF16)],
        compiler_params=_params(),
        cost_estimate=_cost(4 * rows * tokens * width, 4 * rows * width + 2 * tokens * width),
        name="grad_hidden_part",
    )(pos, stats, targets, logit, table, table_oth)

    nxy = lax.axis_size(XY)
    feats = width // nxy
    got = lax.all_to_all(part, XY, 0, 0, tiled=True).reshape(nxy, feats, tokens)
    by_z = pl.pallas_call(
        _sum_kernel,
        in_specs=[smem, pl.BlockSpec(memory_space=pltpu.VMEM)],
        out_specs=pl.BlockSpec(memory_space=pltpu.VMEM),
        out_shape=jax.ShapeDtypeStruct((nz, n_tok, feats), F32),
        compiler_params=_params(),
        cost_estimate=_cost(width * tokens, 2 * width * tokens),
        name="sum_xy",
    )(pos, got)
    by_z = lax.all_to_all(by_z, "z", 0, 0, tiled=True)
    grad_hidden = jnp.sum(by_z, axis=0).astype(BF16)

    dl_oth = lax.ppermute(dl[rows:], "c", swap)
    small = pl.BlockSpec((rows, tokens), _const(0, 0))
    row = pl.BlockSpec((1, 2 * tokens), _const(0, 0))
    grad_table = pl.pallas_call(
        _grad_table_kernel,
        grid=(steps,),
        in_specs=[smem, row, small, small, col(tokens), col(tokens), col(2 * tokens)],
        out_specs=col(rows),
        out_shape=jax.ShapeDtypeStruct((rows, width), BF16),
        scratch_shapes=[pltpu.VMEM((rows, 2 * tokens), BF16)],
        compiler_params=_params(),
        cost_estimate=_cost(8 * rows * tokens * width, 8 * tokens * width + 2 * rows * width),
        name="grad_table",
    )(pos, toks, dl[:rows], dl_oth, h_own, h_oth, e_all)

    loss = loss[0, 0]
    loss = loss + lax.ppermute(loss, "c", swap)
    return grad_hidden, grad_table, loss


def solution(mesh):
    fine = Mesh(mesh.devices.reshape(4, 4, 8, 2), ALL)
    in_specs = (P(("z", "c"), None), P(ALL, None), P(("z", "c"), None), P(("z", "c")), P(("z", "c")))
    out_specs = (P(("z", "c"), XY), P(ALL, None), P())
    return jax.shard_map(per_device, mesh=fine, in_specs=in_specs, out_specs=out_specs, check_vma=False)
```

time: 427 us -> 198 us (0.46)
  blocking collectives: 165 us -> 29.4 us
  waiting for transfers between devices: 207 us -> 74.7 us
  Pallas kernels: 0 us -> 35.8 us
  starting transfers between devices: 0.16 us -> 34.3 us
  matrix products: 31.6 us -> 0 us
    pmax x1 -> x0, blocking collectives: 75.2 us -> none  [per_device(): row_top = lax.pmax(local_top, ('vocab', 'dp'))]
    unnamed x5 -> x1, waiting for transfers between devices: 74.6 us -> 0.02 us
    psum x1 -> x0, blocking collectives: 73.4 us -> none  [per_device(): lax.psum((jnp.sum(shifted, axis=1), local_target), ('vocab', 'dp'))]
    reduce_scatter x1 -> x0, waiting for transfers between devices: 70.9 us -> none  [per_device(): lax.psum_scatter(jnp.dot(dlogits, table, preferred_element_type=jnp.float...]
    all_gather x2 -> x1, waiting for transfers between devices: 61.3 us -> 0.01 us  [per_device(): e_all = lax.all_gather(e_src, ('z', 'c'), axis=0, tiled=True)]
    all_to_all x0 -> x3, waiting for transfers between devices: none -> 45 us  [the longest x1 32 us: per_device(): got = lax.all_to_all(part, XY, 0, 0, tiled=True).reshape(nxy, feats, tokens)]
    pallas_call x0 -> x4, Pallas kernels: none -> 35.8 us  [the longest x1 12 us: per_device(): pl.pallas_call(_grad_table_kernel, grid=(steps,), in_specs=[smem, row, sm...]
    dot_general x4 -> x0, matrix products: 31.6 us -> none  [the longest x1 8.81 us: per_device(): lax.dot_general(onehot_tok, grads_all, (((0,), (0,)), ((), ())), preferre...]
  transfers between devices with their start and end apart: 4 -> 16, of which waited for: 4 -> 9; matrix products, arithmetic and copies ran while one was open for 6% -> 1% of each run, Pallas kernels for 0% -> 12%
where the time goes in v1:
time: 198 us; the launch traced here: 197 us
  waiting for transfers between devices  74.7 us (38%)
  Pallas kernels  35.8 us (18%)
  starting transfers between devices  34.3 us (17%)
  blocking collectives  29.4 us (15%)
  between operations  16.5 us (8%)
  local copies, waits for them, and re-layouts  5.26 us (3%)
    all_to_all x1, waiting for transfers between devices, per_device(): got = lax.all_to_all(part, XY, 0, 0, tiled=True).reshape(nxy, feats, tokens)  32 us
    all_to_all x1, blocking collectives, per_device(): lax.all_to_all(jnp.broadcast_to(payload[None], (peers, 8, lanes)), XYZ, 0...  29.4 us
    ppermute x3, waiting for transfers between devices, per_device(): lax.ppermute(u, 'z', up)  20.6 us
    pallas_call x1, Pallas kernels, per_device(): pl.pallas_call(_grad_table_kernel, grid=(steps,), in_specs=[smem, row, sm...  12 us
    pallas_call x1, Pallas kernels, per_device(): pl.pallas_call(functools.partial(_logits_kernel, steps, rows), grid=(step...  11.7 us
    pallas_call x1, Pallas kernels, per_device(): pl.pallas_call(functools.partial(_grad_hidden_kernel, rows), grid=(steps,...  10.3 us
    all_to_all x1, waiting for transfers between devices, per_device(): by_z = lax.all_to_all(by_z, 'z', 0, 0, tiled=True)  8.78 us
    ppermute x3, starting transfers between devices, per_device(): lax.ppermute(d, 'z', down)  8.68 us
  transfers between devices with their start and end apart: 16, of which 9 were waited for; matrix products, arithmetic and copies ran while one was open for 1% of the time, Pallas kernels for 12%

profile of v1, /device:TPU:8, one launch (start us, length us, event | category | flops | bytes accessed | tf_op | source)
XLA Modules:
  0.0 197.4 jit_solution(3308210912166406784)
XLA Ops:
  7.2 2.0 %collective-permute-start = (bf16[32,5120]{1,0:T(8,128)(2,1)}, bf16[32,5120]{1,0:T(8,128)(2,1)S(1)}, u32[]{:S(2)}, u32[]{:S(2)}) collective-permute-start(bf16[32,5120]{1,0:T(8,128)(2,1)} %refs_0_.1), channel_id=1, source_target_pairs={{0,2},{2,4},{4,6},{6,8},{8,10},{10,12},{12,14},{14,0},{1,3},{3,5},... | collective-permute-start | bytes 983048 | tf_op jit(solution)/shard_map/ppermute | solution.py:139
  9.2 4.0 %collective-permute-start.1 = (bf16[32,5120]{1,0:T(8,128)(2,1)}, bf16[32,5120]{1,0:T(8,128)(2,1)S(1)}, u32[]{:S(2)}, u32[]{:S(2)}) collective-permute-start(bf16[32,5120]{1,0:T(8,128)(2,1)} %refs_0_.1), channel_id=1, source_target_pairs={{0,14},{2,0},{4,2},{6,4},{8,6},{10,8},{12,10},{14,12},{1,15},{3,1}... | collective-permute-start | bytes 983048 | tf_op jit(solution)/shard_map/ppermute | solution.py:139
  13.2 7.8 %collective-permute-done.refs_8_ = bf16[32,5120]{1,0:T(8,128)(2,1)S(1)} collective-permute-done((bf16[32,5120]{1,0:T(8,128)(2,1)}, bf16[32,5120]{1,0:T(8,128)(2,1)S(1)}, u32[]{:S(2)}, u32[]{:S(2)}) %collective-permute-start) | collective-permute-done | bytes 327712 | tf_op jit(solution)/shard_map/ppermute | solution.py:139
  21.1 3.2 %collective-permute-start.3 = (bf16[32,5120]{1,0:T(8,128)(2,1)S(1)}, bf16[32,5120]{1,0:T(8,128)(2,1)S(1)}, u32[]{:S(2)}, u32[]{:S(2)}) collective-permute-start(bf16[32,5120]{1,0:T(8,128)(2,1)S(1)} %collective-permute-done.1.refs_1_), channel_id=1, source_target_pairs={{0,14},{2,0},{4,2},{6,4},{8,6},{10,8},{12,10},{14,12},{1,15},{3,1}... | collective-permute-start | bytes 983048 | tf_op jit(solution)/shard_map/ppermute | solution.py:139
  24.3 6.9 %collective-permute-done.2.refs_7_ = bf16[32,5120]{1,0:T(8,128)(2,1)S(1)} collective-permute-done((bf16[32,5120]{1,0:T(8,128)(2,1)S(1)}, bf16[32,5120]{1,0:T(8,128)(2,1)S(1)}, u32[]{:S(2)}, u32[]{:S(2)}) %collective-permute-start.2) | collective-permute-done | bytes 327712 | tf_op jit(solution)/shard_map/ppermute | solution.py:139
  31.2 1.8 collective-permute-start.4
  34.4 5.9 %collective-permute-done.4.refs_6_ = bf16[32,5120]{1,0:T(8,128)(2,1)S(1)} collective-permute-done((bf16[32,5120]{1,0:T(8,128)(2,1)S(1)}, bf16[32,5120]{1,0:T(8,128)(2,1)S(1)}, u32[]{:S(2)}, u32[]{:S(2)}) %collective-permute-start.4) | collective-permute-done | bytes 327712 | tf_op jit(solution)/shard_map/ppermute | solution.py:139
  40.4 1.6 collective-permute-start.6
  42.0 5.0 %collective-permute-done.6.refs_4_ = bf16[16,5120]{1,0:T(8,128)(2,1)S(1)} collective-permute-done((bf16[16,5120]{1,0:T(8,128)(2,1)S(1)}, bf16[16,5120]{1,0:T(8,128)(2,1)S(1)}, u32[]{:S(2)}, u32[]{:S(2)}) %collective-permute-start.6) | collective-permute-done | bytes 163872 | tf_op jit(solution)/shard_map/ppermute | solution.py:143
  48.5 5.1 %all-to-all-start = ((s32[16,1,64]{2,1,0:T(1,128)}), s32[16,1,64]{2,1,0:T(1,128)S(1)}, u32[]{:S(2)}, u32[]{:S(2)}) async-start(s32[16,1,64]{2,1,0:T(1,128)} %broadcast_in_dim.6), calls=%async_computation | async-start | bytes 16384 | tf_op jit(solution)/shard_map/all_to_all | solution.py:147
  53.6 3.2 %collective-permute-start.7 = (bf16[16,5120]{1,0:T(8,128)(2,1)S(1)}, bf16[16,5120]{1,0:T(8,128)(2,1)S(1)}, u32[]{:S(2)}, u32[]{:S(2)}) collective-permute-start(bf16[16,5120]{1,0:T(8,128)(2,1)S(1)} %slice.23), channel_id=1, source_target_pairs={{0,14},{2,0},{4,2},{6,4},{8,6},{10,8},{12,10},{14,12},{1,15},{3,1}... | collective-permute-start | bytes 491528 | tf_op jit(solution)/shard_map/ppermute | solution.py:143
  56.9 4.2 %all-to-all-done = s32[16,1,64]{2,1,0:T(1,128)S(1)} async-done(((s32[16,1,64]{2,1,0:T(1,128)}), s32[16,1,64]{2,1,0:T(1,128)S(1)}, u32[]{:S(2)}, u32[]{:S(2)}) %all-to-all-start) | async-done | bytes 4128 | tf_op jit(solution)/shard_map/all_to_all | solution.py:147
  61.2 3.0 %collective-permute-done.7.refs_5_ = bf16[16,5120]{1,0:T(8,128)(2,1)S(1)} collective-permute-done((bf16[16,5120]{1,0:T(8,128)(2,1)S(1)}, bf16[16,5120]{1,0:T(8,128)(2,1)S(1)}, u32[]{:S(2)}, u32[]{:S(2)}) %collective-permute-start.7) | collective-permute-done | bytes 163872 | tf_op jit(solution)/shard_map/ppermute | solution.py:143
  65.1 11.7 %logits.1 = (f32[1024,256]{1,0:T(8,128)S(1)}, bf16[256,5120]{1,0:T(8,128)(2,1)}, f32[8,256]{1,0:T(8,128)S(1)}) custom-call(s32[3]{0:T(128)S(1)} %pad_add_fusion.pos_ref, s32[1,256]{1,0:T(1,128)S(1)} %reshape.28.tgt_ref, bf16[32,5120]{1,0:T(8,128)(2,1)S(1)} %copy-done.1, bf16[32,5120]{1,0:T(8,128)(2,1)S(1)} %collective-permute-done.1.refs_1_, ...), custom_call_target="tpu_custom_call" | custom-call | flops 2684354560 | bytes 15728640 | tf_op jit(solution)/shard_map/logits/pallas_call | solution.py:154
  76.9 29.4 %all_to_all.28.stat_ref = f32[128,8,128]{2,1,0:T(8,128)S(1)} all-to-all(f32[128,8,128]{2,1,0:T(8,128)S(1)} %broadcast_in_dim.15), channel_id=1, replica_groups=mesh['x'=4,'y'=4,'z'=8,'c'=2] {'x','y','z'}, dimensions={0} | all-to-all | bytes 1048576 | tf_op jit(solution)/shard_map/all_to_all | solution.py:179
  106.3 10.3 %grad_hidden_part.1 = (bf16[5120,256]{1,0:T(8,128)(2,1)S(1)}, bf16[1024,256]{1,0:T(8,128)(2,1)S(1)}, f32[1,1]{1,0:T(1,128)}) custom-call(s32[3]{0:T(128)S(1)} %pad_add_fusion.pos_ref, f32[128,8,128]{2,1,0:T(8,128)S(1)} %all_to_all.28.stat_ref, s32[1,256]{1,0:T(1,128)S(1)} %reshape.28.tgt_ref, f32[1024,256]{1,0:T(8,128)S(1)} %get-tuple-element.27.logit_ref, ...), custom_call_target="tpu_custom_call" | custom-call | flops 2684354560 | bytes 13107200 | tf_op jit(solution)/shard_map/grad_hidden_part/pallas_call | solution.py:183
  116.7 1.6 copy-done
  118.3 6.7 %all-to-all-start.2 = ((bf16[16,320,256]{2,1,0:T(8,128)(2,1)}), bf16[16,320,256]{2,1,0:T(8,128)(2,1)S(1)}, u32[]{:S(2)}, u32[]{:S(2)}) async-start(bf16[16,320,256]{2,1,0:T(8,128)(2,1)} %bitcast.9), calls=%async_computation.2 | async-start | bytes 5242880 | tf_op jit(solution)/shard_map/all_to_all | solution.py:212
  125.0 32.0 %all-to-all-done.2.got_ref = bf16[16,320,256]{2,1,0:T(8,128)(2,1)S(1)} async-done(((bf16[16,320,256]{2,1,0:T(8,128)(2,1)}), bf16[16,320,256]{2,1,0:T(8,128)(2,1)S(1)}, u32[]{:S(2)}, u32[]{:S(2)}) %all-to-all-start.2) | async-done | bytes 2621472 | tf_op jit(solution)/shard_map/all_to_all | solution.py:212
  157.0 1.8 sum_xy.1
  158.8 4.4 %all-to-all-start.3 = ((f32[8,32,320]{2,1,0:T(8,128)}), f32[8,32,320]{2,1,0:T(8,128)S(1)}, u32[]{:S(2)}, u32[]{:S(2)}) async-start(f32[8,32,320]{2,1,0:T(8,128)} %sum_xy.1), calls=%async_computation.3 | async-start | bytes 786432 | tf_op jit(solution)/shard_map/all_to_all | solution.py:222
  166.2 8.8 %all-to-all-done.3 = f32[8,32,320]{2,1,0:T(8,128)S(1)} async-done(((f32[8,32,320]{2,1,0:T(8,128)}), f32[8,32,320]{2,1,0:T(8,128)S(1)}, u32[]{:S(2)}, u32[]{:S(2)}) %all-to-all-start.3) | async-done | bytes 327712 | tf_op jit(solution)/shard_map/all_to_all | solution.py:222
  175.7 1.7 copy-done.2
  177.4 12.0 %grad_table.1 = bf16[512,5120]{1,0:T(8,128)(2,1)} custom-call(s32[3]{0:T(128)S(1)} %pad_add_fusion.pos_ref, s32[1,512]{1,0:T(1,128)S(1)} %reshape.29.tok_ref, bf16[512,256]{1,0:T(8,128)(2,1)S(1)} %get-tuple-element.34.dl_own_ref, bf16[512,256]{1,0:T(8,128)(2,1)S(1)} %collective-permute-done.9.dl_oth_ref, bf16[256,5120]{1,0:T(8,128)(2,1)S(1)} %copy-done.2, ...), custom_call_target="tpu_custom_call" | custom-call | flops 5368709120 | bytes 15728640 | tf_op jit(solution)/shard_map/grad_table/pallas_call | solution.py:228
  (34 shorter events, 6.7 us)
Async XLA Ops:
  7.2 168.5 %all-gather.2.cloned.1.call-start = ((), (), s32[]{:S(2)}) async-start(), calls=%async_computation.4 | async-start | bytes 5570560 | tf_op jit(solution)/shard_map/all_gather | solution.py:174
  7.2 13.9 %collective-permute-start = (bf16[32,5120]{1,0:T(8,128)(2,1)}, bf16[32,5120]{1,0:T(8,128)(2,1)S(1)}, u32[]{:S(2)}, u32[]{:S(2)}) collective-permute-start(bf16[32,5120]{1,0:T(8,128)(2,1)} %refs_0_.1), channel_id=1, source_target_pairs={{0,2},{2,4},{4,6},{6,8},{8,10},{10,12},{12,14},{14,0},{1,3},{3,5},... | collective-permute-start | bytes 983048 | tf_op jit(solution)/shard_map/ppermute | solution.py:139
  9.2 11.9 %collective-permute-start.1 = (bf16[32,5120]{1,0:T(8,128)(2,1)}, bf16[32,5120]{1,0:T(8,128)(2,1)S(1)}, u32[]{:S(2)}, u32[]{:S(2)}) collective-permute-start(bf16[32,5120]{1,0:T(8,128)(2,1)} %refs_0_.1), channel_id=1, source_target_pairs={{0,14},{2,0},{4,2},{6,4},{8,6},{10,8},{12,10},{14,12},{1,15},{3,1}... | collective-permute-start | bytes 983048 | tf_op jit(solution)/shard_map/ppermute | solution.py:139
  21.1 10.1 %collective-permute-start.2 = (bf16[32,5120]{1,0:T(8,128)(2,1)S(1)}, bf16[32,5120]{1,0:T(8,128)(2,1)S(1)}, u32[]{:S(2)}, u32[]{:S(2)}) collective-permute-start(bf16[32,5120]{1,0:T(8,128)(2,1)S(1)} %collective-permute-done.refs_8_), channel_id=1, source_target_pairs={{0,2},{2,4},{4,6},{6,8},{8,10},{10,12},{12,14},{14,0},{1,3},{3,5},... | collective-permute-start | bytes 983048 | tf_op jit(solution)/shard_map/ppermute | solution.py:139
  21.1 10.1 %collective-permute-start.3 = (bf16[32,5120]{1,0:T(8,128)(2,1)S(1)}, bf16[32,5120]{1,0:T(8,128)(2,1)S(1)}, u32[]{:S(2)}, u32[]{:S(2)}) collective-permute-start(bf16[32,5120]{1,0:T(8,128)(2,1)S(1)} %collective-permute-done.1.refs_1_), channel_id=1, source_target_pairs={{0,14},{2,0},{4,2},{6,4},{8,6},{10,8},{12,10},{14,12},{1,15},{3,1}... | collective-permute-start | bytes 983048 | tf_op jit(solution)/shard_map/ppermute | solution.py:139
  31.2 9.2 %collective-permute-start.4 = (bf16[32,5120]{1,0:T(8,128)(2,1)S(1)}, bf16[32,5120]{1,0:T(8,128)(2,1)S(1)}, u32[]{:S(2)}, u32[]{:S(2)}) collective-permute-start(bf16[32,5120]{1,0:T(8,128)(2,1)S(1)} %collective-permute-done.2.refs_7_), channel_id=1, source_target_pairs={{0,2},{2,4},{4,6},{6,8},{8,10},{10,12},{12,14},{14,0},{1,3},{3,5},... | collective-permute-start | bytes 983048 | tf_op jit(solution)/shard_map/ppermute | solution.py:139
  33.0 7.4 %collective-permute-start.5 = (bf16[32,5120]{1,0:T(8,128)(2,1)S(1)}, bf16[32,5120]{1,0:T(8,128)(2,1)S(1)}, u32[]{:S(2)}, u32[]{:S(2)}) collective-permute-start(bf16[32,5120]{1,0:T(8,128)(2,1)S(1)} %collective-permute-done.3.refs_2_), channel_id=1, source_target_pairs={{0,14},{2,0},{4,2},{6,4},{8,6},{10,8},{12,10},{14,12},{1,15},{3,1}... | collective-permute-start | bytes 983048 | tf_op jit(solution)/shard_map/ppermute | solution.py:139
  40.4 6.6 %collective-permute-start.6 = (bf16[16,5120]{1,0:T(8,128)(2,1)S(1)}, bf16[16,5120]{1,0:T(8,128)(2,1)S(1)}, u32[]{:S(2)}, u32[]{:S(2)}) collective-permute-start(bf16[16,5120]{1,0:T(8,128)(2,1)S(1)} %slice.22), channel_id=1, source_target_pairs={{0,2},{2,4},{4,6},{6,8},{8,10},{10,12},{12,14},{14,0},{1,3},{3,5},... | collective-permute-start | bytes 491528 | tf_op jit(solution)/shard_map/ppermute | solution.py:143
  47.0 17.1 %collective-permute-start.8 = (bf16[512,5120]{1,0:T(8,128)(2,1)}, bf16[512,5120]{1,0:T(8,128)(2,1)}, u32[]{:S(2)}, u32[]{:S(2)}) collective-permute-start(bf16[512,5120]{1,0:T(8,128)(2,1)} %own_ref.1), channel_id=1, source_target_pairs={{0,1},{1,0},{2,3},{3,2},{4,5},{5,4},{6,7},{7,6},{8,9},{9,8},{10,11... | collective-permute-start | bytes 15728648 | tf_op jit(solution)/shard_map/ppermute | solution.py:136
  48.5 12.6 %all-to-all-start = ((s32[16,1,64]{2,1,0:T(1,128)}), s32[16,1,64]{2,1,0:T(1,128)S(1)}, u32[]{:S(2)}, u32[]{:S(2)}) async-start(s32[16,1,64]{2,1,0:T(1,128)} %broadcast_in_dim.6), calls=%async_computation | async-start | bytes 16384 | tf_op jit(solution)/shard_map/all_to_all | solution.py:147
  53.6 10.5 %collective-permute-start.7 = (bf16[16,5120]{1,0:T(8,128)(2,1)S(1)}, bf16[16,5120]{1,0:T(8,128)(2,1)S(1)}, u32[]{:S(2)}, u32[]{:S(2)}) collective-permute-start(bf16[16,5120]{1,0:T(8,128)(2,1)S(1)} %slice.23), channel_id=1, source_target_pairs={{0,14},{2,0},{4,2},{6,4},{8,6},{10,8},{12,10},{14,12},{1,15},{3,1}... | collective-permute-start | bytes 491528 | tf_op jit(solution)/shard_map/ppermute | solution.py:143
  64.2 1.0 copy-start.1
  116.7 1.6 copy-start
  118.3 38.7 %all-to-all-start.2 = ((bf16[16,320,256]{2,1,0:T(8,128)(2,1)}), bf16[16,320,256]{2,1,0:T(8,128)(2,1)S(1)}, u32[]{:S(2)}, u32[]{:S(2)}) async-start(bf16[16,320,256]{2,1,0:T(8,128)(2,1)} %bitcast.9), calls=%async_computation.2 | async-start | bytes 5242880 | tf_op jit(solution)/shard_map/all_to_all | solution.py:212
  125.0 50.7 %collective-permute-start.10 = (bf16[256,5120]{1,0:T(8,128)(2,1)}, bf16[256,5120]{1,0:T(8,128)(2,1)}, u32[]{:S(2)}, u32[]{:S(2)}) collective-permute-start(bf16[256,5120]{1,0:T(8,128)(2,1)} %get-tuple-element.30.h_own_ref), channel_id=1, source_target_pairs={{0,1},{1,0},{2,3},{3,2},{4,5},{5,4},{6,7},{7,6},{8,9},{9,8},{10,11... | collective-permute-start | bytes 7864328 | tf_op jit(solution)/shard_map/ppermute | solution.py:181
  158.8 16.3 %all-to-all-start.3 = ((f32[8,32,320]{2,1,0:T(8,128)}), f32[8,32,320]{2,1,0:T(8,128)S(1)}, u32[]{:S(2)}, u32[]{:S(2)}) async-start(f32[8,32,320]{2,1,0:T(8,128)} %sum_xy.1), calls=%async_computation.3 | async-start | bytes 786432 | tf_op jit(solution)/shard_map/all_to_all | solution.py:222
  163.2 12.5 %collective-permute-start.9 = (bf16[512,256]{1,0:T(8,128)(2,1)S(1)}, bf16[512,256]{1,0:T(8,128)(2,1)S(1)}, u32[]{:S(2)}, u32[]{:S(2)}) collective-permute-start(bf16[512,256]{1,0:T(8,128)(2,1)S(1)} %get-tuple-element.33), channel_id=1, source_target_pairs={{0,1},{1,0},{2,3},{3,2},{4,5},{5,4},{6,7},{7,6},{8,9},{9,8},{10,11... | collective-permute-start | bytes 786440 | tf_op jit(solution)/shard_map/ppermute | solution.py:225
  163.4 1.6 collective-permute-start.11
  175.7 1.7 copy-start.2
Sparse Core Ops, SparseCore 0:
  47.1 43.4 all-gather.1

commit v2 on v0

v2 whole, which is shorter than its diff:
```python
import functools

import jax
import jax.numpy as jnp
from jax import lax
from jax.experimental import pallas as pl
from jax.experimental.pallas import tpu as pltpu
from jax.sharding import Mesh
from jax.sharding import PartitionSpec as P

XY = ("x", "y")
ALL = ("x", "y", "z", "c")
F32 = jnp.float32
BF16 = jnp.bfloat16
LIMIT = 40 * 1024 * 1024
WIDE = 1024
SLOTS = 32
LANES = 256
MORE_SLOTS = 64
NT = (((1,), (1,)), ((), ()))
TN = (((0,), (0,)), ((), ()))


def _params():
    return pltpu.CompilerParams(vmem_limit_bytes=LIMIT)


def _cost(flops, moved):
    return pl.CostEstimate(flops=flops, bytes_accessed=moved, transcendentals=0)


def _row_ids(pos_ref, rows, tokens):
    at = lax.broadcasted_iota(jnp.int32, (2 * rows, tokens), 0)
    return jnp.where(at < rows, pos_ref[1] + at, pos_ref[2] + at - rows)


def _picks(hit, rank_ref, slots, first):
    slot = lax.broadcasted_iota(jnp.int32, (slots, rank_ref.shape[1]), 0) + first
    mine = jnp.where(slot == rank_ref[...], 1.0, 0.0).astype(BF16)
    hot = jnp.where(hit, 1.0, 0.0).astype(BF16)
    return lax.dot_general(mine, hot, NT, preferred_element_type=F32).astype(BF16)


def _thirds(v, count=3):
    rows = []
    for _ in range(count):
        rows.append(v.astype(BF16).astype(F32))
        v = v - rows[-1]
    return rows


def _forward_kernel(rows, pos_ref, tgt_ref, rank_ref, own_hbm, oth_hbm, *refs):
    pieces = refs[:-7]
    logit_ref, hid_hbm, part_hbm, tab, hid, part, sem = refs[-7:]
    tokens, width = hid.shape
    block = pieces[0].shape[0]
    z = pos_ref[0]
    copies = []
    for n, (turn, skip) in enumerate([(0, 0), (1, 0), (2, 0), (3, 0), (4, 0), (4, block // 2), (5, 0), (6, 0), (7, 0)]):
        at = pl.multiple_of(lax.rem(z + turn, 8) * block + skip, block // 2)
        copies.append(pltpu.make_async_copy(pieces[n], hid.at[pl.ds(at, pieces[n].shape[0])], sem.at[n]))
        copies[-1].start()
    n, loads = len(copies), []
    for i in range(width // WIDE):
        cut = pl.ds(i * WIDE, WIDE)
        for k, src in enumerate((own_hbm, oth_hbm)):
            loads.append(pltpu.make_async_copy(src.at[:, cut], tab.at[k, :, cut], sem.at[n]))
            loads[-1].start()
            n += 1
    for c in copies:
        c.wait()
    keep = pltpu.make_async_copy(hid, hid_hbm, sem.at[n])
    keep.start()
    for i in range(width // WIDE):
        cut = pl.ds(i * WIDE, WIDE)
        for k in range(2):
            loads[2 * i + k].wait()
        for k in range(2):
            a = lax.dot_general(tab[k, :, cut], hid[:, cut], NT, preferred_element_type=F32)
            if i == 0:
                logit_ref[pl.ds(k * rows, rows)] = a
            else:
                logit_ref[pl.ds(k * rows, rows)] += a
    logit = logit_ref[...]
    top = jnp.max(logit, axis=0, keepdims=True)
    raised = jnp.exp(logit - top)
    total = jnp.sum(raised, axis=0, keepdims=True)
    hit = _row_ids(pos_ref, rows, tokens) == tgt_ref[...]
    own = jnp.sum(jnp.where(hit, logit, 0.0), axis=0, keepdims=True)
    pick = _picks(hit, rank_ref, SLOTS, 0)
    lhs = jnp.concatenate([jnp.where(hit, 0.0, raised).T.astype(BF16), pick], axis=0)
    stats = jnp.concatenate(_thirds(top) + _thirds(total, 2) + _thirds(own), axis=0)
    feats = width // part.shape[0]
    outs = []
    for i in range(width // (2 * feats)):
        cut = pl.ds(2 * i * feats, 2 * feats)
        p = jnp.dot(lhs[:, :rows], tab[0, :, cut], preferred_element_type=F32)
        p += jnp.dot(lhs[:, rows:], tab[1, :, cut], preferred_element_type=F32)
        sums, q = p[:tokens].T.astype(BF16), p[tokens:]
        for k in range(2):
            part[2 * i + k, :feats] = sums[k * feats : (k + 1) * feats]
            mine = q[:, k * feats : (k + 1) * feats]
            tail = jnp.concatenate([mine[g * 8 : (g + 1) * 8, LANES:] for g in range(SLOTS // 8)], axis=1)
            part[2 * i + k, feats:] = jnp.concatenate([mine[:, :LANES], tail, stats], axis=0).astype(BF16)
        pair = pl.ds(2 * i, 2)
        outs.append(pltpu.make_async_copy(part.at[pair], part_hbm.at[pair], sem.at[n + 1 + i]))
        outs[-1].start()
    keep.wait()
    for c in outs:
        c.wait()


def _target_rows_kernel(rows, pos_ref, tgt_ref, rank_ref, own_ref, oth_ref, out_ref, pick):
    @pl.when(pl.program_id(0) == 0)
    def _():
        hit = _row_ids(pos_ref, rows, tgt_ref.shape[1]) == tgt_ref[...]
        pick[...] = _picks(hit, rank_ref, out_ref.shape[1], pos_ref[3])

    q = jnp.dot(pick[:, :rows], own_ref[...], preferred_element_type=F32)
    q += jnp.dot(pick[:, rows:], oth_ref[...], preferred_element_type=F32)
    feats = out_ref.shape[2]
    for k in range(out_ref.shape[0]):
        out_ref[k] = q[:, k * feats : (k + 1) * feats].astype(BF16)


def _combine_kernel(place_ref, more_ref, got, out_ref):
    peers, _, tokens = got.shape
    feats = more_ref.shape[0]
    place = place_ref[...]
    heads = jnp.concatenate([got[v, feats : feats + SLOTS] for v in range(peers)], axis=0)
    slot = lax.broadcasted_iota(jnp.int32, (peers * SLOTS, tokens), 0)
    hot = jnp.where(slot == place, 1.0, 0.0).astype(BF16)
    first = lax.dot_general(heads, hot, TN, preferred_element_type=F32)
    ends = [got[v, feats + SLOTS :].astype(F32) for v in range(peers)]
    tails = jnp.concatenate([e[:8] for e in ends], axis=0).astype(BF16)
    rest = feats - LANES
    eighth = lax.broadcasted_iota(jnp.int32, (peers * 8, tokens), 0)
    last = 0.0
    for g in range(SLOTS // 8):
        there = (eighth // 8) * SLOTS + g * 8 + eighth % 8
        hot_g = jnp.where(there == place, 1.0, 0.0).astype(BF16)
        last += lax.dot_general(tails[:, g * rest : (g + 1) * rest], hot_g, TN, preferred_element_type=F32)
    targets = jnp.concatenate([first, last], axis=0) + more_ref[...]
    tops = [e[8:9] + e[9:10] + e[10:11] for e in ends]
    top = functools.reduce(jnp.maximum, tops)
    total, hit, acc = 0.0, 0.0, 0.0
    for v in range(peers):
        scale = jnp.exp(tops[v] - top)
        total += (ends[v][11:12] + ends[v][12:13]) * scale
        hit += ends[v][13:14] + ends[v][14:15] + ends[v][15:16]
        acc += got[v, :feats].astype(F32) * scale
    both = jnp.concatenate([acc, targets], axis=0).T.astype(BF16)
    stats = jnp.concatenate(_thirds(top) + _thirds(total) + _thirds(hit) + [jnp.zeros((7, tokens), F32)], axis=0)
    stats = jnp.concatenate([stats, jnp.zeros((16, 2 * feats - tokens), F32)], axis=1).astype(BF16)
    n_tok = out_ref.shape[1] - 16
    for r in range(out_ref.shape[0]):
        out_ref[r, :n_tok] = both[r * n_tok : (r + 1) * n_tok]
        out_ref[r, n_tok:] = stats


def _finish_kernel(pos_ref, got, grad_ref, stat_ref, turned):
    peers, span, _ = got.shape
    n_tok, feats = grad_ref.shape
    tokens = stat_ref.shape[1]
    ends = [got[r, n_tok:, :tokens].astype(F32) for r in range(peers)]
    tops = [e[0:1] + e[1:2] + e[2:3] for e in ends]
    top = functools.reduce(jnp.maximum, tops)
    scales = [jnp.exp(t - top) for t in tops]
    total = sum((e[3:4] + e[4:5] + e[5:6]) * f for e, f in zip(ends, scales))
    hit = sum(e[6:7] + e[7:8] + e[8:9] for e in ends)
    stat_ref[...] = jnp.concatenate([top, total, hit, jnp.zeros((5, tokens), F32)], axis=0)
    inv = 1.0 / total
    rows = [f * inv for f in scales] + [jnp.exp(hit - top) * inv - 1.0, jnp.zeros((128 - peers - 1, tokens), F32)]
    turned[...] = jnp.concatenate(rows, axis=0).T
    own = turned[pl.ds(pl.multiple_of(pos_ref[0] * n_tok, n_tok), n_tok)]
    grad, targets = 0.0, 0.0
    for r in range(peers):
        block = got[r, :n_tok].astype(F32)
        grad += block[:, :feats] * own[:, r : r + 1]
        targets += block[:, feats:]
    grad_ref[...] = (grad + targets * own[:, peers : peers + 1]).astype(BF16)


def _grad_table_kernel(pos_ref, tok_ref, tgt_own, tgt_oth, stat_own, stat_oth, logit_own, logit_oth, h_own, h_oth, e_ref, out_ref, loss_ref, dl, hot):
    @pl.when(pl.program_id(0) == 0)
    def _():
        rows, tokens = logit_own.shape
        at = lax.broadcasted_iota(jnp.int32, hot.shape, 0) + pos_ref[1]
        hot[...] = jnp.where(at == tok_ref[...], 1.0, 0.0).astype(BF16)
        losses = []
        for k, (tgt, stat, logit) in enumerate(((tgt_own, stat_own, logit_own), (tgt_oth, stat_oth, logit_oth))):
            top, total = stat[0:1], stat[1:2]
            hit = jnp.where(at[:, :tokens] == tgt[...], 1.0, 0.0)
            dl[k] = (jnp.exp(logit[...] - top) * (1.0 / total) - hit).astype(BF16)
            losses.append(jnp.sum(top + jnp.log(total) - stat[2:3], keepdims=True))
        loss_ref[...] = losses[0] + losses[1]

    acc = jnp.dot(hot[...], e_ref[...], preferred_element_type=F32)
    acc += jnp.dot(dl[0], h_own[...], preferred_element_type=F32)
    acc += jnp.dot(dl[1], h_oth[...], preferred_element_type=F32)
    out_ref[...] = acc.astype(BF16)


def per_device(hidden, table, embed_grad, token_ids, target_ids):
    rows, width = table.shape
    n_tok = hidden.shape[0]
    nz, nxy = lax.axis_size("z"), lax.axis_size(XY)
    feats = width // nxy
    tokens = n_tok * nz
    xi, yi, zi, ci = (lax.axis_index(a) for a in ALL)
    chip = (xi * 4 + yi) * nz + zi
    swap = [(0, 1), (1, 0)]
    up = [(i, (i + 1) % nz) for i in range(nz)]
    down = [(i, (i - 1) % nz) for i in range(nz)]
    smem = pl.BlockSpec(memory_space=pltpu.SMEM)
    vmem = pl.BlockSpec(memory_space=pltpu.VMEM)
    hbm = pl.BlockSpec(memory_space=pl.ANY)

    def far_off(x):
        return pltpu.with_memory_space_constraint(x, pltpu.HBM)

    def pos_of(first):
        return jnp.stack([zi, (2 * chip + ci) * rows, (2 * chip + 1 - ci) * rows, first]).astype(jnp.int32)

    pos = pos_of(0)
    table_oth = lax.ppermute(table, "c", swap)
    ids = jnp.concatenate([target_ids, token_ids])
    ids = lax.all_to_all(jnp.broadcast_to(ids[None], (2 * nz, 2 * n_tok)), ("z", "c"), 0, 0, tiled=True)

    both = ids[:, :n_tok].reshape(nz, 2, n_tok).transpose(1, 0, 2).reshape(2, tokens)
    owner = both // (2 * rows)
    before = jnp.arange(tokens)[:, None] < jnp.arange(tokens)[None, :]
    ranks = jnp.sum((owner[:, :, None] == owner[:, None, :]) & before[None], axis=1).astype(jnp.int32)
    overflow = jnp.max(ranks) >= SLOTS
    targets = lax.dynamic_index_in_dim(both, ci, 0)
    targets_oth = lax.dynamic_index_in_dim(both, 1 - ci, 0)
    rank = lax.dynamic_index_in_dim(ranks, ci, 0)
    owner = targets // (2 * rows)
    here = owner % nz == zi
    place = jnp.where(here & (rank < SLOTS), owner // nz * SLOTS + rank, -1)
    toks = ids[:, n_tok:].reshape(1, 2 * tokens)

    def round_of(first):
        width_q = 2 * feats
        row = pl.BlockSpec((1, tokens), lambda i: (0, 0))
        sent = pl.pallas_call(
            functools.partial(_target_rows_kernel, rows),
            grid=(width // width_q,),
            in_specs=[smem, row, row, *[pl.BlockSpec((rows, width_q), lambda i: (0, i))] * 2],
            out_specs=pl.BlockSpec((2, MORE_SLOTS, feats), lambda i: (i, 0, 0)),
            out_shape=jax.ShapeDtypeStruct((nxy, MORE_SLOTS, feats), BF16),
            scratch_shapes=[pltpu.VMEM((MORE_SLOTS, 2 * rows), BF16)],
            compiler_params=_params(),
            cost_estimate=_cost(4 * rows * MORE_SLOTS * width, 4 * rows * width),
            name="target_rows",
        )(pos_of(first), targets, rank, table, table_oth)
        got = lax.all_to_all(sent, XY, 0, 0, tiled=True).reshape(nxy * MORE_SLOTS, feats)
        inside = here & (rank >= first) & (rank < first + MORE_SLOTS)
        slot = jnp.where(inside, owner // nz * MORE_SLOTS + rank - first, -1)
        hot = (jnp.arange(nxy * MORE_SLOTS, dtype=jnp.int32)[:, None] == slot).astype(BF16)
        return lax.dot_general(got, hot, TN, preferred_element_type=F32)

    def more():
        return sum(round_of(first) for first in range(SLOTS, tokens, MORE_SLOTS))

    u, d = lax.optimization_barrier((lax.ppermute(hidden, "z", up), lax.ppermute(hidden, "z", down)))
    ups, downs = [u], [d]
    u, d, place, rank, targets, targets_oth, toks = lax.optimization_barrier(
        (lax.ppermute(u, "z", up), lax.ppermute(d, "z", down), place, rank, targets, targets_oth, toks)
    )
    ups.append(u)
    downs.append(d)
    u, d = lax.optimization_barrier((lax.ppermute(u, "z", up), lax.ppermute(d, "z", down)))
    ups.append(u)
    downs.append(d)
    half = n_tok // 2
    q_more = lax.cond(overflow, more, lambda: jnp.zeros((feats, tokens), F32))
    *far, q_more = lax.optimization_barrier((lax.ppermute(u[:half], "z", up), lax.ppermute(d[half:], "z", down), q_more))
    pieces = [hidden, *downs, *far, *ups[::-1]]

    span = feats + SLOTS + 16
    logit, h_own, part = pl.pallas_call(
        functools.partial(_forward_kernel, rows),
        in_specs=[smem, vmem, vmem] + [hbm] * (2 + len(pieces)),
        out_specs=[vmem, hbm, hbm],
        out_shape=[
            jax.ShapeDtypeStruct((2 * rows, tokens), F32),
            pltpu.HBM((tokens, width), BF16),
            pltpu.HBM((nxy, span, tokens), BF16),
        ],
        scratch_shapes=[
            pltpu.VMEM((2, rows, width), BF16),
            pltpu.VMEM((tokens, width), BF16),
            pltpu.VMEM((nxy, span, tokens), BF16),
            pltpu.SemaphoreType.DMA((len(pieces) + 2 * (width // WIDE) + 1 + nxy // 2,)),
        ],
        compiler_params=_params(),
        cost_estimate=_cost(8 * rows * tokens * width, 4 * rows * width + 6 * tokens * width),
        name="forward",
    )(pos, targets, rank, table, table_oth, *pieces)

    e_src, _ = lax.optimization_barrier((embed_grad, far[0]))
    e_all = lax.all_gather(e_src, ("z", "c"), axis=0, tiled=True)

    got = lax.all_to_all(part, XY, 0, 0, tiled=True)
    h_oth = lax.ppermute(h_own, "c", swap)
    logit_oth = lax.ppermute(logit[rows:], "c", swap)

    by_z = pl.pallas_call(
        _combine_kernel,
        in_specs=[vmem] * 3,
        out_specs=vmem,
        out_shape=jax.ShapeDtypeStruct((nz, n_tok + 16, 2 * feats), BF16),
        compiler_params=_params(),
        cost_estimate=_cost(10**6, 10**5),
        name="combine",
    )(place, q_more, got)
    by_z = lax.all_to_all(by_z, "z", 0, 0, tiled=True)

    grad_hidden, stat = pl.pallas_call(
        _finish_kernel,
        in_specs=[smem, vmem],
        out_specs=[vmem, vmem],
        out_shape=[jax.ShapeDtypeStruct((n_tok, feats), BF16), jax.ShapeDtypeStruct((8, tokens), F32)],
        scratch_shapes=[pltpu.VMEM((tokens, 128), F32)],
        compiler_params=_params(),
        cost_estimate=_cost(10**6, 10**5),
        name="finish",
    )(pos, by_z)
    stat_oth = lax.ppermute(stat, "c", swap)

    whole = lambda *shape: pl.BlockSpec(shape, lambda i: (0,) * len(shape))
    col = lambda n: pl.BlockSpec((n, WIDE), lambda i: (0, i))
    grad_table, loss = pl.pallas_call(
        _grad_table_kernel,
        grid=(width // WIDE,),
        in_specs=[smem, whole(1, 2 * tokens), *[whole(1, tokens)] * 2, *[whole(8, tokens)] * 2, *[whole(rows, tokens)] * 2]
        + [col(tokens), col(tokens), col(2 * tokens)],
        out_specs=[col(rows), whole(1, 1)],
        out_shape=[jax.ShapeDtypeStruct((rows, width), BF16), jax.ShapeDtypeStruct((1, 1), F32)],
        scratch_shapes=[pltpu.VMEM((2, rows, tokens), BF16), pltpu.VMEM((rows, 2 * tokens), BF16)],
        compiler_params=_params(),
        cost_estimate=_cost(8 * rows * tokens * width, 8 * tokens * width + 2 * rows * width),
        name="grad_table",
    )(pos, toks, targets, targets_oth, stat, stat_oth, *map(far_off, (logit, logit_oth, h_own, h_oth, e_all)))
    return grad_hidden, grad_table, loss[0, 0]


def solution(mesh):
    fine = Mesh(mesh.devices.reshape(4, 4, 8, 2), ALL)
    in_specs = (P(("z", "c"), None), P(ALL, None), P(("z", "c"), None), P(("z", "c")), P(("z", "c")))
    out_specs = (P(("z", "c"), XY), P(ALL, None), P())
    return jax.shard_map(per_device, mesh=fine, in_specs=in_specs, out_specs=out_specs, check_vma=False)
```

time: 427 us -> 157 us (0.37)
  blocking collectives: 165 us -> 0 us
  waiting for transfers between devices: 207 us -> 75 us
  starting transfers between devices: 0.16 us -> 32.6 us
  matrix products: 31.6 us -> 0 us
  Pallas kernels: 0 us -> 27.2 us
  local copies, waits for them, and re-layouts: 7.48 us -> 2.94 us
    pmax x1 -> x0, blocking collectives: 75.2 us -> none  [per_device(): row_top = lax.pmax(local_top, ('vocab', 'dp'))]
    unnamed x5 -> x1, waiting for transfers between devices: 74.6 us -> 0.02 us
    psum x1 -> x0, blocking collectives: 73.4 us -> none  [per_device(): lax.psum((jnp.sum(shifted, axis=1), local_target), ('vocab', 'dp'))]
    reduce_scatter x1 -> x0, waiting for transfers between devices: 70.9 us -> none  [per_device(): lax.psum_scatter(jnp.dot(dlogits, table, preferred_element_type=jnp.float...]
    all_gather x2 -> x1, waiting for transfers between devices: 61.3 us -> 0.01 us  [per_device(): e_all = lax.all_gather(e_src, ('z', 'c'), axis=0, tiled=True)]
    all_to_all x0 -> x3, waiting for transfers between devices: none -> 55.1 us  [the longest x1 35.1 us: per_device(): got = lax.all_to_all(part, XY, 0, 0, tiled=True)]
    dot_general x4 -> x0, matrix products: 31.6 us -> none  [the longest x1 8.81 us: per_device(): lax.dot_general(onehot_tok, grads_all, (((0,), (0,)), ((), ())), preferre...]
    pallas_call x0 -> x4, Pallas kernels: none -> 27.2 us  [the longest x1 12.9 us: per_device(): pl.pallas_call(functools.partial(_forward_kernel, rows), in_specs=[smem,...]
  transfers between devices with their start and end apart: 4 -> 16, of which waited for: 4 -> 8; matrix products, arithmetic and copies ran while one was open for 6% -> 2% of each run, Pallas kernels for 0% -> 10%
where the time goes in v2:
time: 157 us; the launch traced here: 154 us
  waiting for transfers between devices  75 us (48%)
  starting transfers between devices  32.6 us (21%)
  Pallas kernels  27.2 us (17%)
  between operations  14.8 us (9%)
  local copies, waits for them, and re-layouts  2.94 us (2%)
  other arithmetic  1.68 us (1%)
    all_to_all x1, waiting for transfers between devices, per_device(): got = lax.all_to_all(part, XY, 0, 0, tiled=True)  35.1 us
    ppermute x2, waiting for transfers between devices, per_device(): lax.ppermute(u, 'z', up)  13.7 us
    pallas_call x1, Pallas kernels, per_device(): pl.pallas_call(functools.partial(_forward_kernel, rows), in_specs=[smem,...  12.9 us
    all_to_all x1, waiting for transfers between devices, per_device(): by_z = lax.all_to_all(by_z, 'z', 0, 0, tiled=True)  12.6 us
    pallas_call x1, Pallas kernels, per_device(): pl.pallas_call(_grad_table_kernel, grid=(width // WIDE,), in_specs=[smem,...  11.2 us
    all_to_all x1, waiting for transfers between devices, per_device(): lax.all_to_all(jnp.broadcast_to(ids[None], (2 * nz, 2 * n_tok)), ('z', 'c...  7.41 us
    all_to_all x1, starting transfers between devices, per_device(): got = lax.all_to_all(part, XY, 0, 0, tiled=True)  7.39 us
    ppermute x2, starting transfers between devices, per_device(): lax.ppermute(d, 'z', down)  5.92 us
  transfers between devices with their start and end apart: 16, of which 8 were waited for; matrix products, arithmetic and copies ran while one was open for 2% of the time, Pallas kernels for 10%

profile of v2, /device:TPU:8, one launch (start us, length us, event | category | flops | bytes accessed | tf_op | source)
XLA Modules:
  0.0 154.5 jit_solution(10797891730528531087)
XLA Ops:
  7.3 2.0 %collective-permute-start = (bf16[32,5120]{1,0:T(8,128)(2,1)}, bf16[32,5120]{1,0:T(8,128)(2,1)S(1)}, u32[]{:S(2)}, u32[]{:S(2)}) collective-permute-start(bf16[32,5120]{1,0:T(8,128)(2,1)} %refs_0_.1), channel_id=1, source_target_pairs={{0,2},{2,4},{4,6},{6,8},{8,10},{10,12},{12,14},{14,0},{1,3},{3,5},... | collective-permute-start | bytes 983048 | tf_op jit(solution)/shard_map/ppermute | solution.py:266
  9.3 4.0 %collective-permute-start.1 = (bf16[32,5120]{1,0:T(8,128)(2,1)}, bf16[32,5120]{1,0:T(8,128)(2,1)S(1)}, u32[]{:S(2)}, u32[]{:S(2)}) collective-permute-start(bf16[32,5120]{1,0:T(8,128)(2,1)} %refs_0_.1), channel_id=1, source_target_pairs={{0,14},{2,0},{4,2},{6,4},{8,6},{10,8},{12,10},{14,12},{1,15},{3,1}... | collective-permute-start | bytes 983048 | tf_op jit(solution)/shard_map/ppermute | solution.py:266
  13.3 0.7 pad_add_fusion.6
  14.6 5.9 %all-to-all-start.4 = ((s32[16,1,64]{2,1,0:T(1,128)}), s32[16,1,64]{2,1,0:T(1,128)S(1)}, u32[]{:S(2)}, u32[]{:S(2)}) async-start(s32[16,1,64]{2,1,0:T(1,128)} %broadcast_in_dim.7), calls=%async_computation.4 | async-start | bytes 16384 | tf_op jit(solution)/shard_map/all_to_all | solution.py:228
  20.6 7.4 %all-to-all-done.4 = s32[16,1,64]{2,1,0:T(1,128)S(1)} async-done(((s32[16,1,64]{2,1,0:T(1,128)}), s32[16,1,64]{2,1,0:T(1,128)S(1)}, u32[]{:S(2)}, u32[]{:S(2)}) %all-to-all-start.4) | async-done | bytes 4128 | tf_op jit(solution)/shard_map/all_to_all | solution.py:228
  28.8 2.7 %collective-permute-start.3 = (bf16[32,5120]{1,0:T(8,128)(2,1)S(1)}, bf16[32,5120]{1,0:T(8,128)(2,1)S(1)}, u32[]{:S(2)}, u32[]{:S(2)}) collective-permute-start(bf16[32,5120]{1,0:T(8,128)(2,1)S(1)} %collective-permute-done.1.refs_1_), channel_id=1, source_target_pairs={{0,14},{2,0},{4,2},{6,4},{8,6},{10,8},{12,10},{14,12},{1,15},{3,1}... | collective-permute-start | bytes 983048 | tf_op jit(solution)/shard_map/ppermute | solution.py:269
  31.8 7.2 %collective-permute-done.2.refs_7_ = bf16[32,5120]{1,0:T(8,128)(2,1)S(1)} collective-permute-done((bf16[32,5120]{1,0:T(8,128)(2,1)S(1)}, bf16[32,5120]{1,0:T(8,128)(2,1)S(1)}, u32[]{:S(2)}, u32[]{:S(2)}) %collective-permute-start.2) | collective-permute-done | bytes 327712 | tf_op jit(solution)/shard_map/ppermute | solution.py:269
  38.9 3.2 %collective-permute-start.5 = (bf16[32,5120]{1,0:T(8,128)(2,1)S(1)}, bf16[32,5120]{1,0:T(8,128)(2,1)S(1)}, u32[]{:S(2)}, u32[]{:S(2)}) collective-permute-start(bf16[32,5120]{1,0:T(8,128)(2,1)S(1)} %collective-permute-done.3.refs_2_), channel_id=1, source_target_pairs={{0,14},{2,0},{4,2},{6,4},{8,6},{10,8},{12,10},{14,12},{1,15},{3,1}... | collective-permute-start | bytes 983048 | tf_op jit(solution)/shard_map/ppermute | solution.py:273
  42.2 6.6 %collective-permute-done.4.refs_6_ = bf16[32,5120]{1,0:T(8,128)(2,1)S(1)} collective-permute-done((bf16[32,5120]{1,0:T(8,128)(2,1)S(1)}, bf16[32,5120]{1,0:T(8,128)(2,1)S(1)}, u32[]{:S(2)}, u32[]{:S(2)}) %collective-permute-start.4) | collective-permute-done | bytes 327712 | tf_op jit(solution)/shard_map/ppermute | solution.py:273
  48.8 3.0 %collective-permute-start.7 = (bf16[16,5120]{1,0:T(8,128)(2,1)S(1)}, bf16[16,5120]{1,0:T(8,128)(2,1)S(1)}, u32[]{:S(2)}, u32[]{:S(2)}) collective-permute-start(bf16[16,5120]{1,0:T(8,128)(2,1)S(1)} %slice.18), channel_id=1, source_target_pairs={{0,14},{2,0},{4,2},{6,4},{8,6},{10,8},{12,10},{14,12},{1,15},{3,1}... | collective-permute-start | bytes 491528 | tf_op jit(solution)/shard_map/ppermute | solution.py:278
  51.8 0.6 reduce_max.9
  53.4 1.3 collective-permute-done.7.refs_5_
  54.6 3.7 %collective-permute-done.6.refs_4_ = bf16[16,5120]{1,0:T(8,128)(2,1)S(1)} collective-permute-done((bf16[16,5120]{1,0:T(8,128)(2,1)S(1)}, bf16[16,5120]{1,0:T(8,128)(2,1)S(1)}, u32[]{:S(2)}, u32[]{:S(2)}) %collective-permute-start.6) | collective-permute-done | bytes 163872 | tf_op jit(solution)/shard_map/ppermute | solution.py:278
  58.5 12.9 %forward.1 = (f32[1024,256]{1,0:T(8,128)S(1)}, bf16[256,5120]{1,0:T(8,128)(2,1)}, bf16[16,368,256]{2,1,0:T(8,128)(2,1)}) custom-call(s32[4]{0:T(128)S(1)} %pad_add_fusion.5.pos_ref, s32[1,256]{1,0:T(1,128)S(1)} %get-tuple-element.62.tgt_ref.tgt_own, s32[1,256]{1,0:T(1,128)S(1)} %get-tuple-element.63.rank_ref, bf16[512,5120]{1,0:T(8,128)(2,1)} %own_hbm.1, ...), custom_call_target="tpu_custom_call" | custom-call | flops 5368709120 | bytes 18350080 | tf_op jit(solution)/shard_map/forward/pallas_call | solution.py:282
  71.4 1.0 copy-done
  72.3 7.4 %all-to-all-start.5 = ((bf16[16,368,256]{2,1,0:T(8,128)(2,1)}), bf16[16,368,256]{2,1,0:T(8,128)(2,1)S(1)}, u32[]{:S(2)}, u32[]{:S(2)}) async-start(bf16[16,368,256]{2,1,0:T(8,128)(2,1)} %get-tuple-element.67), calls=%async_computation.5 | async-start | bytes 6029312 | tf_op jit(solution)/shard_map/all_to_all | solution.py:305
  79.7 35.1 %all-to-all-done.5.got = bf16[16,368,256]{2,1,0:T(8,128)(2,1)S(1)} async-done(((bf16[16,368,256]{2,1,0:T(8,128)(2,1)}), bf16[16,368,256]{2,1,0:T(8,128)(2,1)S(1)}, u32[]{:S(2)}, u32[]{:S(2)}) %all-to-all-start.5) | async-done | bytes 3014688 | tf_op jit(solution)/shard_map/all_to_all | solution.py:305
  114.8 1.6 %combine.1 = bf16[8,48,640]{2,1,0:T(8,128)(2,1)} custom-call(s32[1,256]{1,0:T(1,128)S(1)} %get-tuple-element.57.place_ref, f32[320,256]{1,0:T(8,128)S(1)} %get-tuple-element.95.more_ref, bf16[16,368,256]{2,1,0:T(8,128)(2,1)S(1)} %all-to-all-done.5.got), custom_call_target="tpu_custom_call" | custom-call | flops 1000000 | bytes 100000 | tf_op jit(solution)/shard_map/combine/pallas_call | solution.py:309
  116.4 3.5 %all-to-all-start.6 = ((bf16[8,48,640]{2,1,0:T(8,128)(2,1)}), bf16[8,48,640]{2,1,0:T(8,128)(2,1)S(1)}, u32[]{:S(2)}, u32[]{:S(2)}) async-start(bf16[8,48,640]{2,1,0:T(8,128)(2,1)} %combine.1), calls=%async_computation.6 | async-start | bytes 983040 | tf_op jit(solution)/shard_map/all_to_all | solution.py:318
  119.9 1.1 slice.19
  121.1 12.6 %all-to-all-done.6.got = bf16[8,48,640]{2,1,0:T(8,128)(2,1)S(1)} async-done(((bf16[8,48,640]{2,1,0:T(8,128)(2,1)}), bf16[8,48,640]{2,1,0:T(8,128)(2,1)S(1)}, u32[]{:S(2)}, u32[]{:S(2)}) %all-to-all-start.6) | async-done | bytes 491552 | tf_op jit(solution)/shard_map/all_to_all | solution.py:318
  133.8 1.5 finish.1
  135.3 1.2 collective-permute-done.9.stat_oth
  136.4 11.2 %grad_table.1 = (bf16[512,5120]{1,0:T(8,128)(2,1)}, f32[1,1]{1,0:T(1,128)}) custom-call(s32[4]{0:T(128)S(1)} %pad_add_fusion.5.pos_ref, s32[1,512]{1,0:T(1,128)S(1)} %reshape.103.tok_ref, s32[1,256]{1,0:T(1,128)S(1)} %get-tuple-element.62.tgt_ref.tgt_own, s32[1,256]{1,0:T(1,128)S(1)} %get-tuple-element.70.tgt_oth, f32[8,256]{1,0:T(8,128)S(1)} %get-tuple-element.71.stat_own, ...), custom_call_target="tpu_custom_call" | custom-call | flops 5368709120 | bytes 15728640 | tf_op jit(solution)/shard_map/grad_table/pallas_call | solution.py:334
  (36 shorter events, 2.3 us)
Async XLA Ops:
  7.2 45.9 %collective-permute-start.8 = (bf16[512,5120]{1,0:T(8,128)(2,1)}, bf16[512,5120]{1,0:T(8,128)(2,1)}, u32[]{:S(2)}, u32[]{:S(2)}) collective-permute-start(bf16[512,5120]{1,0:T(8,128)(2,1)} %own_hbm.1), channel_id=1, source_target_pairs={{0,1},{1,0},{2,3},{3,2},{4,5},{5,4},{6,7},{7,6},{8,9},{9,8},{10,11... | collective-permute-start | bytes 15728648 | tf_op jit(solution)/shard_map/ppermute | solution.py:226
  7.3 20.9 %collective-permute-start = (bf16[32,5120]{1,0:T(8,128)(2,1)}, bf16[32,5120]{1,0:T(8,128)(2,1)S(1)}, u32[]{:S(2)}, u32[]{:S(2)}) collective-permute-start(bf16[32,5120]{1,0:T(8,128)(2,1)} %refs_0_.1), channel_id=1, source_target_pairs={{0,2},{2,4},{4,6},{6,8},{8,10},{10,12},{12,14},{14,0},{1,3},{3,5},... | collective-permute-start | bytes 983048 | tf_op jit(solution)/shard_map/ppermute | solution.py:266
  9.3 18.9 %collective-permute-start.1 = (bf16[32,5120]{1,0:T(8,128)(2,1)}, bf16[32,5120]{1,0:T(8,128)(2,1)S(1)}, u32[]{:S(2)}, u32[]{:S(2)}) collective-permute-start(bf16[32,5120]{1,0:T(8,128)(2,1)} %refs_0_.1), channel_id=1, source_target_pairs={{0,14},{2,0},{4,2},{6,4},{8,6},{10,8},{12,10},{14,12},{1,15},{3,1}... | collective-permute-start | bytes 983048 | tf_op jit(solution)/shard_map/ppermute | solution.py:266
  14.6 13.4 %all-to-all-start.4 = ((s32[16,1,64]{2,1,0:T(1,128)}), s32[16,1,64]{2,1,0:T(1,128)S(1)}, u32[]{:S(2)}, u32[]{:S(2)}) async-start(s32[16,1,64]{2,1,0:T(1,128)} %broadcast_in_dim.7), calls=%async_computation.4 | async-start | bytes 16384 | tf_op jit(solution)/shard_map/all_to_all | solution.py:228
  20.5 115.9 %all-gather.2.cloned.1.call-start = ((), (), s32[]{:S(2)}) async-start(), calls=%async_computation.7 | async-start | bytes 5570560 | tf_op jit(solution)/shard_map/all_gather | solution.py:303
  28.2 10.8 %collective-permute-start.2 = (bf16[32,5120]{1,0:T(8,128)(2,1)S(1)}, bf16[32,5120]{1,0:T(8,128)(2,1)S(1)}, u32[]{:S(2)}, u32[]{:S(2)}) collective-permute-start(bf16[32,5120]{1,0:T(8,128)(2,1)S(1)} %collective-permute-done.refs_8_), channel_id=1, source_target_pairs={{0,2},{2,4},{4,6},{6,8},{8,10},{10,12},{12,14},{14,0},{1,3},{3,5},... | collective-permute-start | bytes 983048 | tf_op jit(solution)/shard_map/ppermute | solution.py:269
  28.8 10.1 %collective-permute-start.3 = (bf16[32,5120]{1,0:T(8,128)(2,1)S(1)}, bf16[32,5120]{1,0:T(8,128)(2,1)S(1)}, u32[]{:S(2)}, u32[]{:S(2)}) collective-permute-start(bf16[32,5120]{1,0:T(8,128)(2,1)S(1)} %collective-permute-done.1.refs_1_), channel_id=1, source_target_pairs={{0,14},{2,0},{4,2},{6,4},{8,6},{10,8},{12,10},{14,12},{1,15},{3,1}... | collective-permute-start | bytes 983048 | tf_op jit(solution)/shard_map/ppermute | solution.py:269
  38.9 9.8 %collective-permute-start.4 = (bf16[32,5120]{1,0:T(8,128)(2,1)S(1)}, bf16[32,5120]{1,0:T(8,128)(2,1)S(1)}, u32[]{:S(2)}, u32[]{:S(2)}) collective-permute-start(bf16[32,5120]{1,0:T(8,128)(2,1)S(1)} %collective-permute-done.2.refs_7_), channel_id=1, source_target_pairs={{0,2},{2,4},{4,6},{6,8},{8,10},{10,12},{12,14},{14,0},{1,3},{3,5},... | collective-permute-start | bytes 983048 | tf_op jit(solution)/shard_map/ppermute | solution.py:273
  38.9 9.8 %collective-permute-start.5 = (bf16[32,5120]{1,0:T(8,128)(2,1)S(1)}, bf16[32,5120]{1,0:T(8,128)(2,1)S(1)}, u32[]{:S(2)}, u32[]{:S(2)}) collective-permute-start(bf16[32,5120]{1,0:T(8,128)(2,1)S(1)} %collective-permute-done.3.refs_2_), channel_id=1, source_target_pairs={{0,14},{2,0},{4,2},{6,4},{8,6},{10,8},{12,10},{14,12},{1,15},{3,1}... | collective-permute-start | bytes 983048 | tf_op jit(solution)/shard_map/ppermute | solution.py:273
  48.8 5.9 %collective-permute-start.7 = (bf16[16,5120]{1,0:T(8,128)(2,1)S(1)}, bf16[16,5120]{1,0:T(8,128)(2,1)S(1)}, u32[]{:S(2)}, u32[]{:S(2)}) collective-permute-start(bf16[16,5120]{1,0:T(8,128)(2,1)S(1)} %slice.18), channel_id=1, source_target_pairs={{0,14},{2,0},{4,2},{6,4},{8,6},{10,8},{12,10},{14,12},{1,15},{3,1}... | collective-permute-start | bytes 491528 | tf_op jit(solution)/shard_map/ppermute | solution.py:278
  51.8 6.5 %collective-permute-start.6 = (bf16[16,5120]{1,0:T(8,128)(2,1)S(1)}, bf16[16,5120]{1,0:T(8,128)(2,1)S(1)}, u32[]{:S(2)}, u32[]{:S(2)}) collective-permute-start(bf16[16,5120]{1,0:T(8,128)(2,1)S(1)} %slice.17), channel_id=1, source_target_pairs={{0,2},{2,4},{4,6},{6,8},{8,10},{10,12},{12,14},{14,0},{1,3},{3,5},... | collective-permute-start | bytes 491528 | tf_op jit(solution)/shard_map/ppermute | solution.py:278
  53.1 5.3 %copy-start.1 = (bf16[32,5120]{1,0:T(8,128)(2,1)S(1)}, bf16[32,5120]{1,0:T(8,128)(2,1)}, u32[]{:S(2)}) copy-start(bf16[32,5120]{1,0:T(8,128)(2,1)} %refs_0_.1) | copy-start | bytes 983044
  71.4 1.0 copy-start
  72.3 42.5 %all-to-all-start.5 = ((bf16[16,368,256]{2,1,0:T(8,128)(2,1)}), bf16[16,368,256]{2,1,0:T(8,128)(2,1)S(1)}, u32[]{:S(2)}, u32[]{:S(2)}) async-start(bf16[16,368,256]{2,1,0:T(8,128)(2,1)} %get-tuple-element.67), calls=%async_computation.5 | async-start | bytes 6029312 | tf_op jit(solution)/shard_map/all_to_all | solution.py:305
  79.7 55.5 %collective-permute-start.11 = (bf16[256,5120]{1,0:T(8,128)(2,1)}, bf16[256,5120]{1,0:T(8,128)(2,1)}, u32[]{:S(2)}, u32[]{:S(2)}) collective-permute-start(bf16[256,5120]{1,0:T(8,128)(2,1)} %get-tuple-element.73.h_own), channel_id=1, source_target_pairs={{0,1},{1,0},{2,3},{3,2},{4,5},{5,4},{6,7},{7,6},{8,9},{9,8},{10,11... | collective-permute-start | bytes 7864328 | tf_op jit(solution)/shard_map/ppermute | solution.py:306
  116.4 17.3 %all-to-all-start.6 = ((bf16[8,48,640]{2,1,0:T(8,128)(2,1)}), bf16[8,48,640]{2,1,0:T(8,128)(2,1)S(1)}, u32[]{:S(2)}, u32[]{:S(2)}) async-start(bf16[8,48,640]{2,1,0:T(8,128)(2,1)} %combine.1), calls=%async_computation.6 | async-start | bytes 983040 | tf_op jit(solution)/shard_map/all_to_all | solution.py:318
  121.0 14.2 %collective-permute-start.10 = (f32[512,256]{1,0:T(8,128)S(1)}, f32[512,256]{1,0:T(8,128)S(1)}, u32[]{:S(2)}, u32[]{:S(2)}) collective-permute-start(f32[512,256]{1,0:T(8,128)S(1)} %slice.19), channel_id=1, source_target_pairs={{0,1},{1,0},{2,3},{3,2},{4,5},{5,4},{6,7},{7,6},{8,9},{9,8},{10,11... | collective-permute-start | bytes 1572872 | tf_op jit(solution)/shard_map/ppermute | solution.py:307
  135.2 1.2 collective-permute-start.9
  135.2 1.2 copy-start.2
Sparse Core Ops, SparseCore 0:
  58.5 39.5 all-gather.1

commit v3 on v2

v3 whole, which is shorter than its diff:
```python
import functools

import jax
import jax.numpy as jnp
from jax import lax
from jax.experimental import pallas as pl
from jax.experimental.pallas import tpu as pltpu
from jax.sharding import Mesh
from jax.sharding import PartitionSpec as P

XY = ("x", "y")
ALL = ("x", "y", "z", "c")
F32 = jnp.float32
BF16 = jnp.bfloat16
LIMIT = 40 * 1024 * 1024
WIDE = 1024
SLOTS = 8
LANES = 128
MORE_SLOTS = 64
NT = (((1,), (1,)), ((), ()))
TN = (((0,), (0,)), ((), ()))


def _params():
    return pltpu.CompilerParams(vmem_limit_bytes=LIMIT)


def _cost(flops, moved):
    return pl.CostEstimate(flops=flops, bytes_accessed=moved, transcendentals=0)


def _row_ids(pos_ref, rows, tokens):
    at = lax.broadcasted_iota(jnp.int32, (2 * rows, tokens), 0)
    return jnp.where(at < rows, pos_ref[1] + at, pos_ref[2] + at - rows)


def _picks(hit, rank_ref, slots, first):
    slot = lax.broadcasted_iota(jnp.int32, (slots, rank_ref.shape[1]), 0) + first
    mine = jnp.where(slot == rank_ref[...], 1.0, 0.0).astype(BF16)
    hot = jnp.where(hit, 1.0, 0.0).astype(BF16)
    return jnp.minimum(lax.dot_general(mine, hot, NT, preferred_element_type=F32), 1.0).astype(BF16)


def _thirds(v, count=3):
    rows = []
    for _ in range(count):
        rows.append(v.astype(BF16).astype(F32))
        v = v - rows[-1]
    return rows


def _forward_kernel(rows, pos_ref, tgt_ref, rank_ref, own_hbm, oth_hbm, *refs):
    pieces = refs[:-8]
    logit_hbm, hid_hbm, part_hbm, logit_ref, tab, hid, part, sem = refs[-8:]
    tokens, width = hid.shape
    copies, at = [], 0
    for n, p in enumerate(pieces):
        copies.append(pltpu.make_async_copy(p, hid.at[pl.ds(at, p.shape[0])], sem.at[n]))
        copies[-1].start()
        at += p.shape[0]
    n, loads = len(copies), []
    for i in range(width // WIDE):
        cut = pl.ds(i * WIDE, WIDE)
        for k, src in enumerate((own_hbm, oth_hbm)):
            loads.append(pltpu.make_async_copy(src.at[:, cut], tab.at[k, :, cut], sem.at[n]))
            loads[-1].start()
            n += 1
    for c in copies:
        c.wait()
    keep = pltpu.make_async_copy(hid, hid_hbm, sem.at[n])
    keep.start()
    for i in range(width // WIDE):
        cut = pl.ds(i * WIDE, WIDE)
        for k in range(2):
            loads[2 * i + k].wait()
        for k in range(2):
            a = lax.dot_general(tab[k, :, cut], hid[:, cut], NT, preferred_element_type=F32)
            if i == 0:
                logit_ref[pl.ds(k * rows, rows)] = a
            else:
                logit_ref[pl.ds(k * rows, rows)] += a
    held = pltpu.make_async_copy(logit_ref, logit_hbm, sem.at[n + 1])
    held.start()
    logit = logit_ref[...]
    top = jnp.max(logit, axis=0, keepdims=True)
    raised = jnp.exp(logit - top)
    total = jnp.sum(raised, axis=0, keepdims=True)
    hit = _row_ids(pos_ref, rows, tokens) == tgt_ref[...]
    own = jnp.sum(jnp.where(hit, logit, 0.0), axis=0, keepdims=True)
    pick = _picks(hit, rank_ref, SLOTS, 0)
    lhs = jnp.concatenate([jnp.where(hit, 0.0, raised).T.astype(BF16), pick], axis=0)
    stats = jnp.concatenate(_thirds(top) + _thirds(total, 2) + _thirds(own), axis=0)
    feats = width // part.shape[0]
    outs = []
    for i in range(width // (2 * feats)):
        cut = pl.ds(2 * i * feats, 2 * feats)
        p = jnp.dot(lhs[:, :rows], tab[0, :, cut], preferred_element_type=F32)
        p += jnp.dot(lhs[:, rows:], tab[1, :, cut], preferred_element_type=F32)
        sums, q = p[:tokens].T.astype(BF16), p[tokens:]
        for k in range(2):
            part[2 * i + k, :feats] = sums[k * feats : (k + 1) * feats]
            mine = q[:, k * feats : (k + 1) * feats]
            last = jnp.concatenate([mine[:, 2 * LANES :], jnp.zeros((SLOTS, 3 * LANES - feats), F32)], axis=1)
            part[2 * i + k, feats:] = jnp.concatenate([mine[:, :LANES], mine[:, LANES : 2 * LANES], last, stats], axis=0).astype(BF16)
        pair = pl.ds(2 * i, 2)
        outs.append(pltpu.make_async_copy(part.at[pair], part_hbm.at[pair], sem.at[n + 2 + i]))
        outs[-1].start()
    keep.wait()
    held.wait()
    for c in outs:
        c.wait()


def _target_rows_kernel(rows, pos_ref, tgt_ref, rank_ref, own_ref, oth_ref, out_ref, pick):
    @pl.when(pl.program_id(0) == 0)
    def _():
        hit = _row_ids(pos_ref, rows, tgt_ref.shape[1]) == tgt_ref[...]
        pick[...] = _picks(hit, rank_ref, out_ref.shape[1], pos_ref[3])

    q = jnp.dot(pick[:, :rows], own_ref[...], preferred_element_type=F32)
    q += jnp.dot(pick[:, rows:], oth_ref[...], preferred_element_type=F32)
    feats = out_ref.shape[2]
    for k in range(out_ref.shape[0]):
        out_ref[k] = q[:, k * feats : (k + 1) * feats].astype(BF16)


def _summed(place, got, feats):
    peers, _, tokens = got.shape
    slot = lax.broadcasted_iota(jnp.int32, (peers * SLOTS, tokens), 0)
    hot = jnp.where(slot == place, 1.0, 0.0).astype(BF16)
    ends = [got[v, feats:].astype(F32) for v in range(peers)]
    targets = []
    for k in range(3):
        slots = jnp.concatenate([e[k * SLOTS : (k + 1) * SLOTS] for e in ends], axis=0).astype(BF16)
        targets.append(lax.dot_general(slots, hot, TN, preferred_element_type=F32))
    targets = jnp.concatenate(targets, axis=0)[:feats]
    ends = [e[3 * SLOTS :] for e in ends]
    tops = [e[0:1] + e[1:2] + e[2:3] for e in ends]
    top = functools.reduce(jnp.maximum, tops)
    total, hit, acc = 0.0, 0.0, 0.0
    for v in range(peers):
        scale = jnp.exp(tops[v] - top)
        total += (ends[v][3:4] + ends[v][4:5]) * scale
        hit += ends[v][5:6] + ends[v][6:7] + ends[v][7:8]
        acc += got[v, :feats].astype(F32) * scale
    return acc, targets, top, total, hit


def _combine_kernel(pos_ref, place_a, place_b, more_ref, got_a, got_b, out_ref):
    feats, tokens = more_ref.shape
    z = pos_ref[0]
    a, b = _summed(place_a[...], got_a, feats), _summed(place_b[...], got_b, feats)
    acc, targets, top, total, hit = (jnp.concatenate(v, axis=1) for v in zip(a, b))
    both = jnp.concatenate([acc, targets + more_ref[...]], axis=0).T.astype(BF16)
    peers, n_tok = out_ref.shape[0], out_ref.shape[1] - 8
    stats = jnp.concatenate(_thirds(top) + _thirds(total) + _thirds(hit) + [jnp.zeros((7, tokens), F32)], axis=0)
    stats = pltpu.roll(stats, lax.rem(z + peers - 1, peers) * n_tok, 1)
    pairs = [jnp.concatenate([stats[2 * k : 2 * k + 1], stats[2 * k + 1 : 2 * k + 2]], axis=1) for k in range(8)]
    stats = jnp.concatenate(pairs, axis=0)
    stats = jnp.concatenate([stats, jnp.zeros((8, 2 * feats - 2 * tokens), F32)], axis=1).astype(BF16)
    for p in range(peers):
        out_ref[lax.rem(z + p + peers - 1, peers), :n_tok] = both[p * n_tok : (p + 1) * n_tok]
        out_ref[p, n_tok:] = stats


def _finish_kernel(pos_ref, got, grad_ref, stat_ref, turned):
    peers, span, _ = got.shape
    n_tok, feats = grad_ref.shape
    tokens = stat_ref.shape[1]
    wide = [got[r, n_tok:, : 2 * tokens].astype(F32) for r in range(peers)]
    ends = [[w[k // 2 : k // 2 + 1, k % 2 * tokens : (k % 2 + 1) * tokens] for k in range(9)] for w in wide]
    tops = [e[0] + e[1] + e[2] for e in ends]
    top = functools.reduce(jnp.maximum, tops)
    scales = [jnp.exp(t - top) for t in tops]
    total = sum((e[3] + e[4] + e[5]) * f for e, f in zip(ends, scales))
    hit = sum(e[6] + e[7] + e[8] for e in ends)
    stat_ref[...] = jnp.concatenate([top, total, hit, jnp.zeros((5, tokens), F32)], axis=0)
    inv = 1.0 / total
    rows = [f * inv for f in scales] + [jnp.exp(hit - top) * inv - 1.0, jnp.zeros((128 - peers - 1, tokens), F32)]
    turned[...] = jnp.concatenate(rows, axis=0).T
    own = turned[pl.ds(pl.multiple_of(pos_ref[0] * n_tok, n_tok), n_tok)]
    grad, targets = 0.0, 0.0
    for r in range(peers):
        block = got[r, :n_tok].astype(F32)
        grad += block[:, :feats] * own[:, r : r + 1]
        targets += block[:, feats:]
    grad_ref[...] = (grad + targets * own[:, peers : peers + 1]).astype(BF16)


def _grad_table_kernel(pos_ref, tok_ref, tgt_own, tgt_oth, stat_own, stat_oth, *refs):
    own_a, own_b, oth_a, oth_b, h_own_a, h_own_b, h_oth_a, h_oth_b, e_ref, out_ref, loss_ref, dl, hot = refs

    @pl.when(pl.program_id(0) == 0)
    def _():
        rows, tokens = own_a.shape[0], tgt_own.shape[1]
        at = lax.broadcasted_iota(jnp.int32, hot.shape, 0) + pos_ref[1]
        hot[...] = jnp.where(at == tok_ref[...], 1.0, 0.0).astype(BF16)
        turn = lax.rem(9 - pos_ref[0], 8) * (tokens // 8)
        losses = []
        for k, (tgt, stat, a, b) in enumerate(((tgt_own, stat_own, own_a, own_b), (tgt_oth, stat_oth, oth_a, oth_b))):
            losses.append(jnp.sum(stat[0:1] + jnp.log(stat[1:2]) - stat[2:3], keepdims=True))
            turned = pltpu.roll(stat[...], turn, 1)
            hit = jnp.where(at[:, :tokens] == tgt[...], 1.0, 0.0)
            logit = jnp.concatenate([a[...], b[...]], axis=1)
            dl[k] = (jnp.exp(logit - turned[0:1]) * (1.0 / turned[1:2]) - hit).astype(BF16)
        loss_ref[...] = losses[0] + losses[1]

    acc = jnp.dot(hot[...], e_ref[...], preferred_element_type=F32)
    acc += jnp.dot(dl[0], jnp.concatenate([h_own_a[...], h_own_b[...]], axis=0), preferred_element_type=F32)
    acc += jnp.dot(dl[1], jnp.concatenate([h_oth_a[...], h_oth_b[...]], axis=0), preferred_element_type=F32)
    out_ref[...] = acc.astype(BF16)


def per_device(hidden, table, embed_grad, token_ids, target_ids):
    rows, width = table.shape
    n_tok = hidden.shape[0]
    nz, nxy = lax.axis_size("z"), lax.axis_size(XY)
    feats = width // nxy
    tokens = n_tok * nz
    xi, yi, zi, ci = (lax.axis_index(a) for a in ALL)
    chip = (xi * 4 + yi) * nz + zi
    swap = [(0, 1), (1, 0)]
    up = [(i, (i + 1) % nz) for i in range(nz)]
    down = [(i, (i - 1) % nz) for i in range(nz)]
    smem = pl.BlockSpec(memory_space=pltpu.SMEM)
    vmem = pl.BlockSpec(memory_space=pltpu.VMEM)
    hbm = pl.BlockSpec(memory_space=pl.ANY)

    def far_off(x):
        return pltpu.with_memory_space_constraint(x, pltpu.HBM)

    def pos_of(first):
        return jnp.stack([zi, (2 * chip + ci) * rows, (2 * chip + 1 - ci) * rows, first]).astype(jnp.int32)

    pos = pos_of(0)
    table_oth = lax.ppermute(table, "c", swap)
    ids = jnp.concatenate([target_ids, token_ids])
    ids = lax.all_to_all(jnp.broadcast_to(ids[None], (2 * nz, 2 * n_tok)), ("z", "c"), 0, 0, tiled=True)

    u, d = lax.optimization_barrier((lax.ppermute(hidden, "z", up), lax.ppermute(hidden, "z", down)))
    ups, downs = [u], [d]
    u, d, ids = lax.optimization_barrier((lax.ppermute(u, "z", up), lax.ppermute(d, "z", down), ids))
    ups.append(u)
    downs.append(d)

    both = ids[:, :n_tok].reshape(nz, 2, n_tok).transpose(1, 0, 2)
    both = jnp.roll(both, 1 - zi, axis=1).reshape(2, tokens)
    part_of = jnp.arange(tokens) // (tokens // 2)
    alike = part_of[:, None] == part_of[None, :]
    before = jnp.arange(tokens)[:, None] < jnp.arange(tokens)[None, :]
    same = both[:, :, None] == both[:, None, :]
    fresh = ~jnp.any(same & (alike & before)[None], axis=1)
    owner = both // (2 * rows)
    below = (owner[:, :, None] == owner[:, None, :]) & (both[:, :, None] < both[:, None, :]) & alike[None] & fresh[:, :, None]
    ranks = jnp.sum(below, axis=1).astype(jnp.int32)
    overflow = jnp.max(ranks) >= SLOTS
    targets = lax.dynamic_index_in_dim(both, ci, 0)
    targets_oth = lax.dynamic_index_in_dim(both, 1 - ci, 0)
    rank = lax.dynamic_index_in_dim(ranks, ci, 0)
    owner = targets // (2 * rows)
    here = owner % nz == zi
    place = jnp.where(here & (rank < SLOTS), owner // nz * SLOTS + rank, -1)
    toks = ids[:, n_tok:].reshape(1, 2 * tokens)

    def round_of(first, part):
        rank_in = jnp.where(part_of[None] == part, rank, -1)
        width_q = 2 * feats
        row = pl.BlockSpec((1, tokens), lambda i: (0, 0))
        sent = pl.pallas_call(
            functools.partial(_target_rows_kernel, rows),
            grid=(width // width_q,),
            in_specs=[smem, row, row, *[pl.BlockSpec((rows, width_q), lambda i: (0, i))] * 2],
            out_specs=pl.BlockSpec((2, MORE_SLOTS, feats), lambda i: (i, 0, 0)),
            out_shape=jax.ShapeDtypeStruct((nxy, MORE_SLOTS, feats), BF16),
            scratch_shapes=[pltpu.VMEM((MORE_SLOTS, 2 * rows), BF16)],
            compiler_params=_params(),
            cost_estimate=_cost(4 * rows * MORE_SLOTS * width, 4 * rows * width),
            name="target_rows",
        )(pos_of(first), targets, rank_in, table, table_oth)
        got = lax.all_to_all(sent, XY, 0, 0, tiled=True).reshape(nxy * MORE_SLOTS, feats)
        inside = here & (rank_in >= first) & (rank_in < first + MORE_SLOTS)
        slot = jnp.where(inside, owner // nz * MORE_SLOTS + rank_in - first, -1)
        hot = (jnp.arange(nxy * MORE_SLOTS, dtype=jnp.int32)[:, None] == slot).astype(BF16)
        return lax.dot_general(got, hot, TN, preferred_element_type=F32)

    def more():
        return sum(round_of(first, part) for part in range(2) for first in range(SLOTS, tokens // 2, MORE_SLOTS))

    span = feats + 3 * SLOTS + 8
    wide = tokens // 2

    def forward(name, part, share, *pieces):
        cut = slice(part * wide, (part + 1) * wide)
        return pl.pallas_call(
            functools.partial(_forward_kernel, rows),
            in_specs=[smem, vmem, vmem] + [hbm] * (2 + len(pieces)),
            out_specs=[hbm] * 3,
            out_shape=[
                pltpu.HBM((2 * rows, wide), F32),
                pltpu.HBM((wide, width), BF16),
                pltpu.HBM((nxy, span, wide), BF16),
            ],
            scratch_shapes=[
                pltpu.VMEM((2 * rows, wide), F32),
                pltpu.VMEM((2, rows, width), BF16),
                pltpu.VMEM((wide, width), BF16),
                pltpu.VMEM((nxy, span, wide), BF16),
                pltpu.SemaphoreType.DMA((len(pieces) + 2 * (width // WIDE) + 2 + nxy // 2,)),
            ],
            compiler_params=_params(),
            cost_estimate=_cost(8 * rows * wide * width // share, (4 * rows * width + 6 * wide * width) // share),
            name=name,
        )(pos, targets[:, cut], rank[:, cut], table, table_oth, *pieces)

    half = n_tok // 2
    u2, d2 = u, d
    u, d = lax.ppermute(u2, "z", up), lax.ppermute(d2, "z", down)
    far = (
        lax.ppermute(u2[:half], "z", [(i, (i + 2) % nz) for i in range(nz)]),
        lax.ppermute(d2[half:], "z", [(i, (i - 2) % nz) for i in range(nz)]),
    )
    logit_a, h_own_a, part_a = forward("forward_a", 0, 1, ups[0], far_off(hidden), downs[0], downs[1])
    q_more = lax.cond(overflow, more, lambda: jnp.zeros((feats, tokens), F32))
    u, d, *far, part_a, q_more = lax.optimization_barrier((u, d, *far, part_a, q_more))
    got_a = lax.all_to_all(part_a, XY, 0, 0, tiled=True)
    logit_b, h_own_b, part_b = forward("forward_b", 1, 1, d, *far, u, ups[1])
    got_b = lax.all_to_all(part_b, XY, 0, 0, tiled=True)

    e_src, _ = lax.optimization_barrier((embed_grad, far[0]))
    e_all = lax.all_gather(e_src, ("z", "c"), axis=0, tiled=True)

    h_oth_a, h_oth_b, oth_a, oth_b = (
        lax.ppermute(v, "c", swap) for v in (h_own_a, h_own_b, logit_a[rows:], logit_b[rows:])
    )
    place_a, place_b = place[:, :wide], place[:, wide:]

    by_z = pl.pallas_call(
        _combine_kernel,
        in_specs=[smem] + [vmem] * 5,
        out_specs=vmem,
        out_shape=jax.ShapeDtypeStruct((nz, n_tok + 8, 2 * feats), BF16),
        compiler_params=_params(),
        cost_estimate=_cost(10**6, 10**5),
        name="combine",
    )(pos, place_a, place_b, q_more, got_a, got_b)
    by_z = lax.all_to_all(by_z, "z", 0, 0, tiled=True)

    grad_hidden, stat = pl.pallas_call(
        _finish_kernel,
        in_specs=[smem, vmem],
        out_specs=[vmem, vmem],
        out_shape=[jax.ShapeDtypeStruct((n_tok, feats), BF16), jax.ShapeDtypeStruct((8, tokens), F32)],
        scratch_shapes=[pltpu.VMEM((tokens, 128), F32)],
        compiler_params=_params(),
        cost_estimate=_cost(10**6, 10**5),
        name="finish",
    )(pos, by_z)
    stat_oth = lax.ppermute(stat, "c", swap)

    whole = lambda *shape: pl.BlockSpec(shape, lambda i: (0,) * len(shape))
    col = lambda n: pl.BlockSpec((n, WIDE), lambda i: (0, i))
    grad_table, loss = pl.pallas_call(
        _grad_table_kernel,
        grid=(width // WIDE,),
        in_specs=[smem, whole(1, 2 * tokens), *[whole(1, tokens)] * 2, *[whole(8, tokens)] * 2, *[whole(rows, wide)] * 4]
        + [col(wide)] * 4
        + [col(2 * tokens)],
        out_specs=[col(rows), whole(1, 1)],
        out_shape=[jax.ShapeDtypeStruct((rows, width), BF16), jax.ShapeDtypeStruct((1, 1), F32)],
        scratch_shapes=[pltpu.VMEM((2, rows, tokens), BF16), pltpu.VMEM((rows, 2 * tokens), BF16)],
        compiler_params=_params(),
        cost_estimate=_cost(8 * rows * tokens * width, 8 * tokens * width + 2 * rows * width),
        name="grad_table",
    )(pos, toks, targets, targets_oth, stat, stat_oth, logit_a, logit_b, oth_a, oth_b, *map(far_off, (h_own_a, h_own_b, h_oth_a, h_oth_b, e_all)))
    return grad_hidden, grad_table, loss[0, 0]


def solution(mesh):
    fine = Mesh(mesh.devices.reshape(4, 4, 8, 2), ALL)
    in_specs = (P(("z", "c"), None), P(ALL, None), P(("z", "c"), None), P(("z", "c")), P(("z", "c")))
    out_specs = (P(("z", "c"), XY), P(ALL, None), P())
    return jax.shard_map(per_device, mesh=fine, in_specs=in_specs, out_specs=out_specs, check_vma=False)
```

time: 157 us -> 144 us (0.917)
  waiting for transfers between devices: 75 us -> 48.2 us
  starting transfers between devices: 32.6 us -> 40.4 us
  Pallas kernels: 27.2 us -> 34.9 us
  local copies, waits for them, and re-layouts: 2.94 us -> 1.02 us
    ppermute x2 -> x1, waiting for transfers between devices: 13.7 us -> 4.44 us  [per_device(): lax.ppermute(u, 'z', up)]
    all_to_all x1 -> x2, waiting for transfers between devices: 35.1 us -> 26.3 us  [the longest x1 18.8 us: per_device(): got_b = lax.all_to_all(part_b, XY, 0, 0, tiled=True)]
    pallas_call x2 -> x3, Pallas kernels: 14.5 us -> 22.7 us  [the longest x2 20.1 us: forward(): pl.pallas_call(functools.partial(_forward_kernel, rows), in_specs=[smem,...]
    all_to_all x1 -> x2, starting transfers between devices: 7.39 us -> 12.3 us  [the longest x1 7.4 us: per_device(): got_a = lax.all_to_all(part_a, XY, 0, 0, tiled=True)]
    ppermute x4 -> x8, starting transfers between devices: 3.13 us -> 7.71 us  [the longest x2 3.39 us: per_device(): u, d = (lax.ppermute(u2, 'z', up), lax.ppermute(d2, 'z', down))]
    all_to_all x1, waiting for transfers between devices: 7.41 us -> 2.89 us  [per_device(): lax.all_to_all(jnp.broadcast_to(ids[None], (2 * nz, 2 * n_tok)), ('z', 'c...]
    ppermute x4 -> x8, waiting for transfers between devices: 4.99 us -> 1.19 us  [the longest x1 1.17 us: per_device(): lax.ppermute(d2[half:], 'z', [(i, (i - 2) % nz) for i in range(nz)])]
    ppermute x2 -> x1, starting transfers between devices: 5.92 us -> 2.32 us  [per_device(): lax.ppermute(d, 'z', down)]
  transfers between devices with their start and end apart: 16 -> 19, of which waited for: 8 -> 8; matrix products, arithmetic and copies ran while one was open for 2% -> 2% of each run, Pallas kernels for 10% -> 17%
where the time goes in v3:
time: 144 us; the launch traced here: 142 us
  waiting for transfers between devices  48.2 us (33%)
  starting transfers between devices  40.4 us (28%)
  Pallas kernels  34.9 us (24%)
  between operations  14.9 us (10%)
  other arithmetic  2.11 us (1%)
    pallas_call x2, Pallas kernels, forward(): pl.pallas_call(functools.partial(_forward_kernel, rows), in_specs=[smem,...  20.1 us
    all_to_all x1, waiting for transfers between devices, per_device(): got_b = lax.all_to_all(part_b, XY, 0, 0, tiled=True)  18.8 us
    all_to_all x1, waiting for transfers between devices, per_device(): by_z = lax.all_to_all(by_z, 'z', 0, 0, tiled=True)  11.2 us
    pallas_call x1, Pallas kernels, per_device(): pl.pallas_call(_grad_table_kernel, grid=(width // WIDE,), in_specs=[smem,...  10.7 us
    all_to_all x1, waiting for transfers between devices, per_device(): got_a = lax.all_to_all(part_a, XY, 0, 0, tiled=True)  7.56 us
    all_to_all x1, starting transfers between devices, per_device(): got_a = lax.all_to_all(part_a, XY, 0, 0, tiled=True)  7.4 us
    all_to_all x1, starting transfers between devices, per_device(): lax.all_to_all(jnp.broadcast_to(ids[None], (2 * nz, 2 * n_tok)), ('z', 'c...  5.86 us
    all_to_all x1, starting transfers between devices, per_device(): by_z = lax.all_to_all(by_z, 'z', 0, 0, tiled=True)  5.2 us
  transfers between devices with their start and end apart: 19, of which 8 were waited for; matrix products, arithmetic and copies ran while one was open for 2% of the time, Pallas kernels for 17%

profile of v3, /device:TPU:8, one launch (start us, length us, event | category | flops | bytes accessed | tf_op | source)
XLA Modules:
  0.0 141.8 jit_solution(7132021747323750855)
XLA Ops:
  7.3 2.0 %collective-permute-start = (bf16[32,5120]{1,0:T(8,128)(2,1)}, bf16[32,5120]{1,0:T(8,128)(2,1)S(1)}, u32[]{:S(2)}, u32[]{:S(2)}) collective-permute-start(bf16[32,5120]{1,0:T(8,128)(2,1)} %refs_1_.1), channel_id=1, source_target_pairs={{0,2},{2,4},{4,6},{6,8},{8,10},{10,12},{12,14},{14,0},{1,3},{3,5},... | collective-permute-start | bytes 983048 | tf_op jit(solution)/shard_map/ppermute | solution.py:240
  9.3 4.0 %collective-permute-start.1 = (bf16[32,5120]{1,0:T(8,128)(2,1)}, bf16[32,5120]{1,0:T(8,128)(2,1)S(1)}, u32[]{:S(2)}, u32[]{:S(2)}) collective-permute-start(bf16[32,5120]{1,0:T(8,128)(2,1)} %refs_1_.1), channel_id=1, source_target_pairs={{0,14},{2,0},{4,2},{6,4},{8,6},{10,8},{12,10},{14,12},{1,15},{3,1}... | collective-permute-start | bytes 983048 | tf_op jit(solution)/shard_map/ppermute | solution.py:240
  14.6 5.9 %all-to-all-start.4 = ((s32[16,1,64]{2,1,0:T(1,128)}), s32[16,1,64]{2,1,0:T(1,128)S(1)}, u32[]{:S(2)}, u32[]{:S(2)}) async-start(s32[16,1,64]{2,1,0:T(1,128)} %broadcast_in_dim.13), calls=%async_computation.4 | async-start | bytes 16384 | tf_op jit(solution)/shard_map/all_to_all | solution.py:238
  20.6 1.1 collective-permute-done.refs_0_
  22.6 2.3 %collective-permute-start.3 = (bf16[32,5120]{1,0:T(8,128)(2,1)S(1)}, bf16[32,5120]{1,0:T(8,128)(2,1)S(1)}, u32[]{:S(2)}, u32[]{:S(2)}) collective-permute-start(bf16[32,5120]{1,0:T(8,128)(2,1)S(1)} %collective-permute-done.1.refs_2_), channel_id=1, source_target_pairs={{0,14},{2,0},{4,2},{6,4},{8,6},{10,8},{12,10},{14,12},{1,15},{3,1}... | collective-permute-start | bytes 983048 | tf_op jit(solution)/shard_map/ppermute | solution.py:242
  25.2 2.9 %all-to-all-done.4 = s32[16,1,64]{2,1,0:T(1,128)S(1)} async-done(((s32[16,1,64]{2,1,0:T(1,128)}), s32[16,1,64]{2,1,0:T(1,128)S(1)}, u32[]{:S(2)}, u32[]{:S(2)}) %all-to-all-start.4) | async-done | bytes 4128 | tf_op jit(solution)/shard_map/all_to_all | solution.py:238
  28.0 4.4 %collective-permute-done.2.refs_4_ = bf16[32,5120]{1,0:T(8,128)(2,1)S(1)} collective-permute-done((bf16[32,5120]{1,0:T(8,128)(2,1)S(1)}, bf16[32,5120]{1,0:T(8,128)(2,1)S(1)}, u32[]{:S(2)}, u32[]{:S(2)}) %collective-permute-start.2) | collective-permute-done | bytes 327712 | tf_op jit(solution)/shard_map/ppermute | solution.py:242
  32.5 2.0 %collective-permute-start.4 = (bf16[32,5120]{1,0:T(8,128)(2,1)S(1)}, bf16[32,5120]{1,0:T(8,128)(2,1)S(1)}, u32[]{:S(2)}, u32[]{:S(2)}) collective-permute-start(bf16[32,5120]{1,0:T(8,128)(2,1)S(1)} %collective-permute-done.2.refs_4_), channel_id=1, source_target_pairs={{0,2},{2,4},{4,6},{6,8},{8,10},{10,12},{12,14},{14,0},{1,3},{3,5},... | collective-permute-start | bytes 983048 | tf_op jit(solution)/shard_map/ppermute | solution.py:317
  34.5 1.4 %collective-permute-start.5 = (bf16[32,5120]{1,0:T(8,128)(2,1)S(1)}, bf16[32,5120]{1,0:T(8,128)(2,1)S(1)}, u32[]{:S(2)}, u32[]{:S(2)}) collective-permute-start(bf16[32,5120]{1,0:T(8,128)(2,1)S(1)} %collective-permute-done.3.refs_3_), channel_id=1, source_target_pairs={{0,14},{2,0},{4,2},{6,4},{8,6},{10,8},{12,10},{14,12},{1,15},{3,1}... | collective-permute-start | bytes 983048 | tf_op jit(solution)/shard_map/ppermute | solution.py:317
  37.9 1.4 collective-permute-start.7
  39.2 1.6 %collective-permute-start.6 = (bf16[16,5120]{1,0:T(8,128)(2,1)S(1)}, bf16[16,5120]{1,0:T(8,128)(2,1)S(1)}, u32[]{:S(2)}, u32[]{:S(2)}) collective-permute-start(bf16[16,5120]{1,0:T(8,128)(2,1)S(1)} %slice.39), channel_id=1, source_target_pairs={{0,4},{2,6},{4,8},{6,10},{8,12},{10,14},{12,0},{14,2},{1,5},{3,7},... | collective-permute-start | bytes 491528 | tf_op jit(solution)/shard_map/ppermute | solution.py:319
  41.2 9.7 %forward_a.1 = (f32[1024,128]{1,0:T(8,128)}, bf16[128,5120]{1,0:T(8,128)(2,1)}, bf16[16,352,128]{2,1,0:T(8,128)(2,1)}) custom-call(s32[4]{0:T(128)S(1)} %pad_add_fusion.3.pos_ref, s32[1,128]{1,0:T(1,128)S(1)} %get-tuple-element.128.tgt_ref, s32[1,128]{1,0:T(1,128)S(1)} %get-tuple-element.121.rank_ref, bf16[512,5120]{1,0:T(8,128)(2,1)} %own_hbm.3, ...), custom_call_target="tpu_custom_call" | custom-call | flops 2684354560 | bytes 14417920 | tf_op jit(solution)/shard_map/forward_a/pallas_call | solution.py:294
  51.0 1.2 collective-permute-done.7.refs_2_
  52.2 7.4 %all-to-all-start.5 = ((bf16[16,352,128]{2,1,0:T(8,128)(2,1)}), bf16[16,352,128]{2,1,0:T(8,128)(2,1)S(1)}, u32[]{:S(2)}, u32[]{:S(2)}) async-start(bf16[16,352,128]{2,1,0:T(8,128)(2,1)} %get-tuple-element.89), calls=%async_computation.5 | async-start | bytes 2883584 | tf_op jit(solution)/shard_map/all_to_all | solution.py:325
  59.6 10.4 %forward_b.1 = (f32[1024,128]{1,0:T(8,128)}, bf16[128,5120]{1,0:T(8,128)(2,1)}, bf16[16,352,128]{2,1,0:T(8,128)(2,1)}) custom-call(s32[4]{0:T(128)S(1)} %pad_add_fusion.3.pos_ref, s32[1,128]{1,0:T(1,128)S(1)} %get-tuple-element.129.tgt_ref, s32[1,128]{1,0:T(1,128)S(1)} %get-tuple-element.120.rank_ref, bf16[512,5120]{1,0:T(8,128)(2,1)} %own_hbm.3, ...), custom_call_target="tpu_custom_call" | custom-call | flops 2684354560 | bytes 14417920 | tf_op jit(solution)/shard_map/forward_b/pallas_call | solution.py:294
  70.0 7.6 %all-to-all-done.5.got_a = bf16[16,352,128]{2,1,0:T(8,128)(2,1)S(1)} async-done(((bf16[16,352,128]{2,1,0:T(8,128)(2,1)}), bf16[16,352,128]{2,1,0:T(8,128)(2,1)S(1)}, u32[]{:S(2)}, u32[]{:S(2)}) %all-to-all-start.5) | async-done | bytes 1441824 | tf_op jit(solution)/shard_map/all_to_all | solution.py:325
  77.6 4.9 %all-to-all-start.6 = ((bf16[16,352,128]{2,1,0:T(8,128)(2,1)}), bf16[16,352,128]{2,1,0:T(8,128)(2,1)S(1)}, u32[]{:S(2)}, u32[]{:S(2)}) async-start(bf16[16,352,128]{2,1,0:T(8,128)(2,1)} %get-tuple-element.94), calls=%async_computation.6 | async-start | bytes 2883584 | tf_op jit(solution)/shard_map/all_to_all | solution.py:327
  82.9 18.8 %all-to-all-done.6.got_b = bf16[16,352,128]{2,1,0:T(8,128)(2,1)S(1)} async-done(((bf16[16,352,128]{2,1,0:T(8,128)(2,1)}), bf16[16,352,128]{2,1,0:T(8,128)(2,1)S(1)}, u32[]{:S(2)}, u32[]{:S(2)}) %all-to-all-start.6) | async-done | bytes 1441824 | tf_op jit(solution)/shard_map/all_to_all | solution.py:327
  101.7 2.6 %combine.1 = bf16[8,40,640]{2,1,0:T(8,128)(2,1)} custom-call(s32[4]{0:T(128)S(1)} %pad_add_fusion.3.pos_ref, s32[1,128]{1,0:T(1,128)S(1)} %get-tuple-element.125.place_a, s32[1,128]{1,0:T(1,128)S(1)} %get-tuple-element.124.place_b, f32[320,256]{1,0:T(8,128)} %copy-done.2, bf16[16,352,128]{2,1,0:T(8,128)(2,1)S(1)} %all-to-all-done.5.got_a, ...), custom_call_target="tpu_custom_call" | custom-call | flops 1000000 | bytes 100000 | tf_op jit(solution)/shard_map/combine/pallas_call | solution.py:337
  104.3 5.2 %all-to-all-start.7 = ((bf16[8,40,640]{2,1,0:T(8,128)(2,1)}), bf16[8,40,640]{2,1,0:T(8,128)(2,1)S(1)}, u32[]{:S(2)}, u32[]{:S(2)}) async-start(bf16[8,40,640]{2,1,0:T(8,128)(2,1)} %combine.1), calls=%async_computation.7 | async-start | bytes 819200 | tf_op jit(solution)/shard_map/all_to_all | solution.py:346
  110.4 11.2 %all-to-all-done.7.got = bf16[8,40,640]{2,1,0:T(8,128)(2,1)S(1)} async-done(((bf16[8,40,640]{2,1,0:T(8,128)(2,1)}), bf16[8,40,640]{2,1,0:T(8,128)(2,1)S(1)}, u32[]{:S(2)}, u32[]{:S(2)}) %all-to-all-start.7) | async-done | bytes 409632 | tf_op jit(solution)/shard_map/all_to_all | solution.py:346
  121.6 1.5 %finish.1 = (bf16[32,320]{1,0:T(8,128)(2,1)}, f32[8,256]{1,0:T(8,128)S(1)}) custom-call(s32[4]{0:T(128)S(1)} %pad_add_fusion.3.pos_ref, bf16[8,40,640]{2,1,0:T(8,128)(2,1)S(1)} %all-to-all-done.7.got), custom_call_target="tpu_custom_call" | custom-call | flops 1000000 | bytes 100000 | tf_op jit(solution)/shard_map/finish/pallas_call | solution.py:348
  123.1 1.1 collective-permute-done.9.stat_oth
  124.2 10.7 %grad_table.1 = (bf16[512,5120]{1,0:T(8,128)(2,1)}, f32[1,1]{1,0:T(1,128)}) custom-call(s32[4]{0:T(128)S(1)} %pad_add_fusion.3.pos_ref, s32[1,512]{1,0:T(1,128)S(1)} %reshape.190.tok_ref, s32[1,256]{1,0:T(1,128)S(1)} %get-tuple-element.115.tgt_own, s32[1,256]{1,0:T(1,128)S(1)} %get-tuple-element.119.tgt_oth, f32[8,256]{1,0:T(8,128)S(1)} %get-tuple-element.96.stat_own, ...), custom_call_target="tpu_custom_call" | custom-call | flops 5368709120 | bytes 15728640 | tf_op jit(solution)/shard_map/grad_table/pallas_call | solution.py:362
  (52 shorter events, 5.7 us)
Async XLA Ops:
  7.2 33.8 %collective-permute-start.8 = (bf16[512,5120]{1,0:T(8,128)(2,1)}, bf16[512,5120]{1,0:T(8,128)(2,1)}, u32[]{:S(2)}, u32[]{:S(2)}) collective-permute-start(bf16[512,5120]{1,0:T(8,128)(2,1)} %own_hbm.3), channel_id=1, source_target_pairs={{0,1},{1,0},{2,3},{3,2},{4,5},{5,4},{6,7},{7,6},{8,9},{9,8},{10,11... | collective-permute-start | bytes 15728648 | tf_op jit(solution)/shard_map/ppermute | solution.py:236
  7.3 14.4 %collective-permute-start = (bf16[32,5120]{1,0:T(8,128)(2,1)}, bf16[32,5120]{1,0:T(8,128)(2,1)S(1)}, u32[]{:S(2)}, u32[]{:S(2)}) collective-permute-start(bf16[32,5120]{1,0:T(8,128)(2,1)} %refs_1_.1), channel_id=1, source_target_pairs={{0,2},{2,4},{4,6},{6,8},{8,10},{10,12},{12,14},{14,0},{1,3},{3,5},... | collective-permute-start | bytes 983048 | tf_op jit(solution)/shard_map/ppermute | solution.py:240
  9.3 12.4 %collective-permute-start.1 = (bf16[32,5120]{1,0:T(8,128)(2,1)}, bf16[32,5120]{1,0:T(8,128)(2,1)S(1)}, u32[]{:S(2)}, u32[]{:S(2)}) collective-permute-start(bf16[32,5120]{1,0:T(8,128)(2,1)} %refs_1_.1), channel_id=1, source_target_pairs={{0,14},{2,0},{4,2},{6,4},{8,6},{10,8},{12,10},{14,12},{1,15},{3,1}... | collective-permute-start | bytes 983048 | tf_op jit(solution)/shard_map/ppermute | solution.py:240
  14.6 13.4 %all-to-all-start.4 = ((s32[16,1,64]{2,1,0:T(1,128)}), s32[16,1,64]{2,1,0:T(1,128)S(1)}, u32[]{:S(2)}, u32[]{:S(2)}) async-start(s32[16,1,64]{2,1,0:T(1,128)} %broadcast_in_dim.13), calls=%async_computation.4 | async-start | bytes 16384 | tf_op jit(solution)/shard_map/all_to_all | solution.py:238
  20.5 103.7 %all-gather.2.cloned.1.call-start = ((), (), s32[]{:S(2)}) async-start(), calls=%async_computation.8 | async-start | bytes 5570560 | tf_op jit(solution)/shard_map/all_gather | solution.py:330
  21.7 10.8 %collective-permute-start.2 = (bf16[32,5120]{1,0:T(8,128)(2,1)S(1)}, bf16[32,5120]{1,0:T(8,128)(2,1)S(1)}, u32[]{:S(2)}, u32[]{:S(2)}) collective-permute-start(bf16[32,5120]{1,0:T(8,128)(2,1)S(1)} %collective-permute-done.refs_0_), channel_id=1, source_target_pairs={{0,2},{2,4},{4,6},{6,8},{8,10},{10,12},{12,14},{14,0},{1,3},{3,5},... | collective-permute-start | bytes 983048 | tf_op jit(solution)/shard_map/ppermute | solution.py:242
  22.6 9.9 %collective-permute-start.3 = (bf16[32,5120]{1,0:T(8,128)(2,1)S(1)}, bf16[32,5120]{1,0:T(8,128)(2,1)S(1)}, u32[]{:S(2)}, u32[]{:S(2)}) collective-permute-start(bf16[32,5120]{1,0:T(8,128)(2,1)S(1)} %collective-permute-done.1.refs_2_), channel_id=1, source_target_pairs={{0,14},{2,0},{4,2},{6,4},{8,6},{10,8},{12,10},{14,12},{1,15},{3,1}... | collective-permute-start | bytes 983048 | tf_op jit(solution)/shard_map/ppermute | solution.py:242
  32.5 19.7 %collective-permute-start.4 = (bf16[32,5120]{1,0:T(8,128)(2,1)S(1)}, bf16[32,5120]{1,0:T(8,128)(2,1)S(1)}, u32[]{:S(2)}, u32[]{:S(2)}) collective-permute-start(bf16[32,5120]{1,0:T(8,128)(2,1)S(1)} %collective-permute-done.2.refs_4_), channel_id=1, source_target_pairs={{0,2},{2,4},{4,6},{6,8},{8,10},{10,12},{12,14},{14,0},{1,3},{3,5},... | collective-permute-start | bytes 983048 | tf_op jit(solution)/shard_map/ppermute | solution.py:317
  34.5 17.7 %collective-permute-start.5 = (bf16[32,5120]{1,0:T(8,128)(2,1)S(1)}, bf16[32,5120]{1,0:T(8,128)(2,1)S(1)}, u32[]{:S(2)}, u32[]{:S(2)}) collective-permute-start(bf16[32,5120]{1,0:T(8,128)(2,1)S(1)} %collective-permute-done.3.refs_3_), channel_id=1, source_target_pairs={{0,14},{2,0},{4,2},{6,4},{8,6},{10,8},{12,10},{14,12},{1,15},{3,1}... | collective-permute-start | bytes 983048 | tf_op jit(solution)/shard_map/ppermute | solution.py:317
  37.9 14.3 %collective-permute-start.7 = (bf16[16,5120]{1,0:T(8,128)(2,1)S(1)}, bf16[16,5120]{1,0:T(8,128)(2,1)S(1)}, u32[]{:S(2)}, u32[]{:S(2)}) collective-permute-start(bf16[16,5120]{1,0:T(8,128)(2,1)S(1)} %slice.40), channel_id=1, source_target_pairs={{0,12},{2,14},{4,0},{6,2},{8,4},{10,6},{12,8},{14,10},{1,13},{3,15... | collective-permute-start | bytes 491528 | tf_op jit(solution)/shard_map/ppermute | solution.py:320
  39.2 12.9 %collective-permute-start.6 = (bf16[16,5120]{1,0:T(8,128)(2,1)S(1)}, bf16[16,5120]{1,0:T(8,128)(2,1)S(1)}, u32[]{:S(2)}, u32[]{:S(2)}) collective-permute-start(bf16[16,5120]{1,0:T(8,128)(2,1)S(1)} %slice.39), channel_id=1, source_target_pairs={{0,4},{2,6},{4,8},{6,10},{8,12},{10,14},{12,0},{14,2},{1,5},{3,7},... | collective-permute-start | bytes 491528 | tf_op jit(solution)/shard_map/ppermute | solution.py:319
  41.2 9.8 %copy-start.2 = (f32[320,256]{1,0:T(8,128)}, f32[320,256]{1,0:T(8,128)S(1)}, u32[]{:S(2)}) copy-start(f32[320,256]{1,0:T(8,128)S(1)} %get-tuple-element.130.more_ref) | copy-start | bytes 983044
  52.2 25.4 %all-to-all-start.5 = ((bf16[16,352,128]{2,1,0:T(8,128)(2,1)}), bf16[16,352,128]{2,1,0:T(8,128)(2,1)S(1)}, u32[]{:S(2)}, u32[]{:S(2)}) async-start(bf16[16,352,128]{2,1,0:T(8,128)(2,1)} %get-tuple-element.89), calls=%async_computation.5 | async-start | bytes 2883584 | tf_op jit(solution)/shard_map/all_to_all | solution.py:325
  77.6 24.2 %all-to-all-start.6 = ((bf16[16,352,128]{2,1,0:T(8,128)(2,1)}), bf16[16,352,128]{2,1,0:T(8,128)(2,1)S(1)}, u32[]{:S(2)}, u32[]{:S(2)}) async-start(bf16[16,352,128]{2,1,0:T(8,128)(2,1)} %get-tuple-element.94), calls=%async_computation.6 | async-start | bytes 2883584 | tf_op jit(solution)/shard_map/all_to_all | solution.py:327
  82.4 40.7 %collective-permute-start.13 = (bf16[128,5120]{1,0:T(8,128)(2,1)}, bf16[128,5120]{1,0:T(8,128)(2,1)}, u32[]{:S(2)}, u32[]{:S(2)}) collective-permute-start(bf16[128,5120]{1,0:T(8,128)(2,1)} %get-tuple-element.100.refs_5_), channel_id=1, source_target_pairs={{0,1},{1,0},{2,3},{3,2},{4,5},{5,4},{6,7},{7,6},{8,9},{9,8},{10,11... | collective-permute-start | bytes 3932168 | tf_op jit(solution)/shard_map/ppermute | solution.py:333
  82.4 40.7 %collective-permute-start.12 = (bf16[128,5120]{1,0:T(8,128)(2,1)}, bf16[128,5120]{1,0:T(8,128)(2,1)}, u32[]{:S(2)}, u32[]{:S(2)}) collective-permute-start(bf16[128,5120]{1,0:T(8,128)(2,1)} %get-tuple-element.99.refs_4_), channel_id=1, source_target_pairs={{0,1},{1,0},{2,3},{3,2},{4,5},{5,4},{6,7},{7,6},{8,9},{9,8},{10,11... | collective-permute-start | bytes 3932168 | tf_op jit(solution)/shard_map/ppermute | solution.py:333
  101.7 7.8 %copy-start.1 = (f32[1024,128]{1,0:T(8,128)S(1)}, f32[1024,128]{1,0:T(8,128)}, u32[]{:S(2)}) copy-start(f32[1024,128]{1,0:T(8,128)} %get-tuple-element.98.refs_1_) | copy-start | bytes 1572868
  104.3 5.2 %copy-start = (f32[1024,128]{1,0:T(8,128)S(1)}, f32[1024,128]{1,0:T(8,128)}, u32[]{:S(2)}) copy-start(f32[1024,128]{1,0:T(8,128)} %get-tuple-element.97.refs_0_) | copy-start | bytes 1572868
  104.3 17.3 %all-to-all-start.7 = ((bf16[8,40,640]{2,1,0:T(8,128)(2,1)}), bf16[8,40,640]{2,1,0:T(8,128)(2,1)S(1)}, u32[]{:S(2)}, u32[]{:S(2)}) async-start(bf16[8,40,640]{2,1,0:T(8,128)(2,1)} %combine.1), calls=%async_computation.7 | async-start | bytes 819200 | tf_op jit(solution)/shard_map/all_to_all | solution.py:346
  109.6 13.5 %collective-permute-start.10 = (f32[512,128]{1,0:T(8,128)S(1)}, f32[512,128]{1,0:T(8,128)S(1)}, u32[]{:S(2)}, u32[]{:S(2)}) collective-permute-start(f32[512,128]{1,0:T(8,128)S(1)} %slice.46), channel_id=1, source_target_pairs={{0,1},{1,0},{2,3},{3,2},{4,5},{5,4},{6,7},{7,6},{8,9},{9,8},{10,11... | collective-permute-start | bytes 786440 | tf_op jit(solution)/shard_map/ppermute | solution.py:333
  109.9 13.2 %collective-permute-start.11 = (f32[512,128]{1,0:T(8,128)S(1)}, f32[512,128]{1,0:T(8,128)S(1)}, u32[]{:S(2)}, u32[]{:S(2)}) collective-permute-start(f32[512,128]{1,0:T(8,128)S(1)} %slice.47), channel_id=1, source_target_pairs={{0,1},{1,0},{2,3},{3,2},{4,5},{5,4},{6,7},{7,6},{8,9},{9,8},{10,11... | collective-permute-start | bytes 786440 | tf_op jit(solution)/shard_map/ppermute | solution.py:333
  123.0 1.2 collective-permute-start.9
Sparse Core Ops, SparseCore 0:
  52.3 43.1 all-gather.1

commit v4 on v3

--- a/solution.py
+++ b/solution.py
@@ -14,6 +14,7 @@
 BF16 = jnp.bfloat16
 LIMIT = 40 * 1024 * 1024
 WIDE = 1024
+TABLE_WIDE = 1280
 SLOTS = 8
 LANES = 128
 MORE_SLOTS = 64
@@ -146,12 +147,20 @@
     return acc, targets, top, total, hit
 
 
-def _combine_kernel(pos_ref, place_a, place_b, more_ref, got_a, got_b, out_ref):
-    feats, tokens = more_ref.shape
+def _half_kernel(place_ref, got_ref, sums_ref, stat_ref):
+    acc, targets, top, total, hit = _summed(place_ref[...], got_ref, sums_ref.shape[1] // 2)
+    sums_ref[...] = jnp.concatenate([acc, targets], axis=0).T.astype(BF16)
+    stat_ref[...] = jnp.concatenate([top, total, hit, jnp.zeros((5, top.shape[1]), F32)], axis=0)
+
+
+def _combine_kernel(pos_ref, place_ref, more_ref, got_ref, first_ref, stat_ref, out_ref):
     z = pos_ref[0]
-    a, b = _summed(place_a[...], got_a, feats), _summed(place_b[...], got_b, feats)
-    acc, targets, top, total, hit = (jnp.concatenate(v, axis=1) for v in zip(a, b))
-    both = jnp.concatenate([acc, targets + more_ref[...]], axis=0).T.astype(BF16)
+    acc, targets, *rows = _summed(place_ref[...], got_ref, more_ref.shape[0])
+    rest = jnp.concatenate([acc, targets], axis=0).T.astype(BF16)
+    both = jnp.concatenate([first_ref[...], rest], axis=0)
+    feats, tokens = acc.shape[0], both.shape[0]
+    both = both + jnp.concatenate([jnp.zeros((feats, tokens), F32), more_ref[...]], axis=0).T.astype(BF16)
+    top, total, hit = (jnp.concatenate([stat_ref[k : k + 1], v], axis=1) for k, v in enumerate(rows))
     peers, n_tok = out_ref.shape[0], out_ref.shape[1] - 8
     stats = jnp.concatenate(_thirds(top) + _thirds(total) + _thirds(hit) + [jnp.zeros((7, tokens), F32)], axis=0)
     stats = pltpu.roll(stats, lax.rem(z + peers - 1, peers) * n_tok, 1)
@@ -313,27 +322,34 @@
         )(pos, targets[:, cut], rank[:, cut], table, table_oth, *pieces)
 
     half = n_tok // 2
-    u2, d2 = u, d
-    u, d = lax.ppermute(u2, "z", up), lax.ppermute(d2, "z", down)
     far = (
-        lax.ppermute(u2[:half], "z", [(i, (i + 2) % nz) for i in range(nz)]),
-        lax.ppermute(d2[half:], "z", [(i, (i - 2) % nz) for i in range(nz)]),
+        lax.ppermute(u[:half], "z", [(i, (i + 2) % nz) for i in range(nz)]),
+        lax.ppermute(d[half:], "z", [(i, (i - 2) % nz) for i in range(nz)]),
     )
+    u, d = lax.ppermute(u, "z", up), lax.ppermute(d, "z", down)
     logit_a, h_own_a, part_a = forward("forward_a", 0, 1, ups[0], far_off(hidden), downs[0], downs[1])
-    q_more = lax.cond(overflow, more, lambda: jnp.zeros((feats, tokens), F32))
-    u, d, *far, part_a, q_more = lax.optimization_barrier((u, d, *far, part_a, q_more))
+    u, d, *far, part_a = lax.optimization_barrier((u, d, *far, part_a))
     got_a = lax.all_to_all(part_a, XY, 0, 0, tiled=True)
     logit_b, h_own_b, part_b = forward("forward_b", 1, 1, d, *far, u, ups[1])
     got_b = lax.all_to_all(part_b, XY, 0, 0, tiled=True)
 
-    e_src, _ = lax.optimization_barrier((embed_grad, far[0]))
+    e_src, _ = lax.optimization_barrier((embed_grad, u))
     e_all = lax.all_gather(e_src, ("z", "c"), axis=0, tiled=True)
 
     h_oth_a, h_oth_b, oth_a, oth_b = (
         lax.ppermute(v, "c", swap) for v in (h_own_a, h_own_b, logit_a[rows:], logit_b[rows:])
     )
-    place_a, place_b = place[:, :wide], place[:, wide:]
-
+    sums_a, stat_a = pl.pallas_call(
+        _half_kernel,
+        in_specs=[vmem] * 2,
+        out_specs=[vmem] * 2,
+        out_shape=[jax.ShapeDtypeStruct((wide, 2 * feats), BF16), jax.ShapeDtypeStruct((8, wide), F32)],
+        compiler_params=_params(),
+        cost_estimate=_cost(10**6, 10**5),
+        name="half",
+    )(place[:, :wide], got_a)
+    overflow, sums_a, got_b = lax.optimization_barrier((overflow, sums_a, got_b))
+    q_more = lax.cond(overflow, more, lambda: jnp.zeros((feats, tokens), F32))
     by_z = pl.pallas_call(
         _combine_kernel,
         in_specs=[smem] + [vmem] * 5,
@@ -342,7 +358,7 @@
         compiler_params=_params(),
         cost_estimate=_cost(10**6, 10**5),
         name="combine",
-    )(pos, place_a, place_b, q_more, got_a, got_b)
+    )(pos, place[:, wide:], q_more, got_b, sums_a, stat_a)
     by_z = lax.all_to_all(by_z, "z", 0, 0, tiled=True)
 
     grad_hidden, stat = pl.pallas_call(
@@ -358,10 +374,10 @@
     stat_oth = lax.ppermute(stat, "c", swap)
 
     whole = lambda *shape: pl.BlockSpec(shape, lambda i: (0,) * len(shape))
-    col = lambda n: pl.BlockSpec((n, WIDE), lambda i: (0, i))
+    col = lambda n: pl.BlockSpec((n, TABLE_WIDE), lambda i: (0, i))
     grad_table, loss = pl.pallas_call(
         _grad_table_kernel,
-        grid=(width // WIDE,),
+        grid=(width // TABLE_WIDE,),
         in_specs=[smem, whole(1, 2 * tokens), *[whole(1, tokens)] * 2, *[whole(8, tokens)] * 2, *[whole(rows, wide)] * 4]
         + [col(wide)] * 4
         + [col(2 * tokens)],

time: 144 us -> 143 us (level)
  waiting for transfers between devices: 48.2 us -> 43.8 us
  local copies, waits for them, and re-layouts: 1.02 us -> 3.47 us
  starting transfers between devices: 40.4 us -> 42.4 us
    all_to_all x1, waiting for transfers between devices: 18.8 us -> 15.9 us  [per_device(): got_b = lax.all_to_all(part_b, XY, 0, 0, tiled=True)]
    unnamed x6 -> x12, local copies, waits for them, and re-layouts: 0.01 us -> 2.46 us
    all_to_all x1, waiting for transfers between devices: 7.56 us -> 5.57 us  [per_device(): got_a = lax.all_to_all(part_a, XY, 0, 0, tiled=True)]
    pallas_call x1 -> x2, Pallas kernels: 10.7 us -> 10.7 us  [the longest x1 10.3 us: per_device(): pl.pallas_call(_grad_table_kernel, grid=(width // TABLE_WIDE,), in_specs=...]
where the time goes in v4:
time: 143 us; the launch traced here: 141 us
  waiting for transfers between devices  43.8 us (31%)
  starting transfers between devices  42.4 us (30%)
  Pallas kernels  33.9 us (24%)
  between operations  14.9 us (10%)
  local copies, waits for them, and re-layouts  3.47 us (2%)
  other arithmetic  2.11 us (1%)
    pallas_call x2, Pallas kernels, forward(): pl.pallas_call(functools.partial(_forward_kernel, rows), in_specs=[smem,...  19.9 us
    all_to_all x1, waiting for transfers between devices, per_device(): got_b = lax.all_to_all(part_b, XY, 0, 0, tiled=True)  15.9 us
    all_to_all x1, waiting for transfers between devices, per_device(): by_z = lax.all_to_all(by_z, 'z', 0, 0, tiled=True)  11.3 us
    pallas_call x1, Pallas kernels, per_device(): pl.pallas_call(_grad_table_kernel, grid=(width // TABLE_WIDE,), in_specs=...  10.3 us
    all_to_all x1, starting transfers between devices, per_device(): got_a = lax.all_to_all(part_a, XY, 0, 0, tiled=True)  7.39 us
    all_to_all x1, starting transfers between devices, per_device(): by_z = lax.all_to_all(by_z, 'z', 0, 0, tiled=True)  6.05 us
    all_to_all x1, starting transfers between devices, per_device(): lax.all_to_all(jnp.broadcast_to(ids[None], (2 * nz, 2 * n_tok)), ('z', 'c...  5.86 us
    all_to_all x1, waiting for transfers between devices, per_device(): got_a = lax.all_to_all(part_a, XY, 0, 0, tiled=True)  5.57 us
  transfers between devices with their start and end apart: 19, of which 8 were waited for; matrix products, arithmetic and copies ran while one was open for 2% of the time, Pallas kernels for 17%

profile of v4, /device:TPU:8, one launch (start us, length us, event | category | flops | bytes accessed | tf_op | source)
XLA Modules:
  0.0 140.8 jit_solution(14863557003508291584)
XLA Ops:
  7.3 2.0 %collective-permute-start = (bf16[32,5120]{1,0:T(8,128)(2,1)}, bf16[32,5120]{1,0:T(8,128)(2,1)S(1)}, u32[]{:S(2)}, u32[]{:S(2)}) collective-permute-start(bf16[32,5120]{1,0:T(8,128)(2,1)} %refs_1_.1), channel_id=1, source_target_pairs={{0,2},{2,4},{4,6},{6,8},{8,10},{10,12},{12,14},{14,0},{1,3},{3,5},... | collective-permute-start | bytes 983048 | tf_op jit(solution)/shard_map/ppermute | solution.py:249
  9.3 4.0 %collective-permute-start.1 = (bf16[32,5120]{1,0:T(8,128)(2,1)}, bf16[32,5120]{1,0:T(8,128)(2,1)S(1)}, u32[]{:S(2)}, u32[]{:S(2)}) collective-permute-start(bf16[32,5120]{1,0:T(8,128)(2,1)} %refs_1_.1), channel_id=1, source_target_pairs={{0,14},{2,0},{4,2},{6,4},{8,6},{10,8},{12,10},{14,12},{1,15},{3,1}... | collective-permute-start | bytes 983048 | tf_op jit(solution)/shard_map/ppermute | solution.py:249
  14.6 5.9 %all-to-all-start.4 = ((s32[16,1,64]{2,1,0:T(1,128)}), s32[16,1,64]{2,1,0:T(1,128)S(1)}, u32[]{:S(2)}, u32[]{:S(2)}) async-start(s32[16,1,64]{2,1,0:T(1,128)} %broadcast_in_dim.13), calls=%async_computation.4 | async-start | bytes 16384 | tf_op jit(solution)/shard_map/all_to_all | solution.py:247
  20.6 1.1 collective-permute-done.refs_0_
  22.6 2.3 %collective-permute-start.3 = (bf16[32,5120]{1,0:T(8,128)(2,1)S(1)}, bf16[32,5120]{1,0:T(8,128)(2,1)S(1)}, u32[]{:S(2)}, u32[]{:S(2)}) collective-permute-start(bf16[32,5120]{1,0:T(8,128)(2,1)S(1)} %collective-permute-done.1.refs_2_), channel_id=1, source_target_pairs={{0,14},{2,0},{4,2},{6,4},{8,6},{10,8},{12,10},{14,12},{1,15},{3,1}... | collective-permute-start | bytes 983048 | tf_op jit(solution)/shard_map/ppermute | solution.py:251
  25.2 2.9 %all-to-all-done.4 = s32[16,1,64]{2,1,0:T(1,128)S(1)} async-done(((s32[16,1,64]{2,1,0:T(1,128)}), s32[16,1,64]{2,1,0:T(1,128)S(1)}, u32[]{:S(2)}, u32[]{:S(2)}) %all-to-all-start.4) | async-done | bytes 4128 | tf_op jit(solution)/shard_map/all_to_all | solution.py:247
  28.0 4.4 %collective-permute-done.2.refs_4_ = bf16[32,5120]{1,0:T(8,128)(2,1)S(1)} collective-permute-done((bf16[32,5120]{1,0:T(8,128)(2,1)S(1)}, bf16[32,5120]{1,0:T(8,128)(2,1)S(1)}, u32[]{:S(2)}, u32[]{:S(2)}) %collective-permute-start.2) | collective-permute-done | bytes 327712 | tf_op jit(solution)/shard_map/ppermute | solution.py:251
  32.5 1.9 %collective-permute-start.4 = (bf16[32,5120]{1,0:T(8,128)(2,1)S(1)}, bf16[32,5120]{1,0:T(8,128)(2,1)S(1)}, u32[]{:S(2)}, u32[]{:S(2)}) collective-permute-start(bf16[32,5120]{1,0:T(8,128)(2,1)S(1)} %collective-permute-done.2.refs_4_), channel_id=1, source_target_pairs={{0,2},{2,4},{4,6},{6,8},{8,10},{10,12},{12,14},{14,0},{1,3},{3,5},... | collective-permute-start | bytes 983048 | tf_op jit(solution)/shard_map/ppermute | solution.py:329
  34.4 1.4 %collective-permute-start.5 = (bf16[32,5120]{1,0:T(8,128)(2,1)S(1)}, bf16[32,5120]{1,0:T(8,128)(2,1)S(1)}, u32[]{:S(2)}, u32[]{:S(2)}) collective-permute-start(bf16[32,5120]{1,0:T(8,128)(2,1)S(1)} %collective-permute-done.3.refs_3_), channel_id=1, source_target_pairs={{0,14},{2,0},{4,2},{6,4},{8,6},{10,8},{12,10},{14,12},{1,15},{3,1}... | collective-permute-start | bytes 983048 | tf_op jit(solution)/shard_map/ppermute | solution.py:329
  36.2 2.7 %collective-permute-start.6 = (bf16[16,5120]{1,0:T(8,128)(2,1)S(1)}, bf16[16,5120]{1,0:T(8,128)(2,1)S(1)}, u32[]{:S(2)}, u32[]{:S(2)}) collective-permute-start(bf16[16,5120]{1,0:T(8,128)(2,1)S(1)} %slice.39), channel_id=1, source_target_pairs={{0,4},{2,6},{4,8},{6,10},{8,12},{10,14},{12,0},{14,2},{1,5},{3,7},... | collective-permute-start | bytes 491528 | tf_op jit(solution)/shard_map/ppermute | solution.py:326
  38.9 1.5 %collective-permute-start.7 = (bf16[16,5120]{1,0:T(8,128)(2,1)S(1)}, bf16[16,5120]{1,0:T(8,128)(2,1)S(1)}, u32[]{:S(2)}, u32[]{:S(2)}) collective-permute-start(bf16[16,5120]{1,0:T(8,128)(2,1)S(1)} %slice.40), channel_id=1, source_target_pairs={{0,12},{2,14},{4,0},{6,2},{8,4},{10,6},{12,8},{14,10},{1,13},{3,15... | collective-permute-start | bytes 491528 | tf_op jit(solution)/shard_map/ppermute | solution.py:327
  40.8 9.8 %forward_a.1 = (f32[1024,128]{1,0:T(8,128)}, bf16[128,5120]{1,0:T(8,128)(2,1)}, bf16[16,352,128]{2,1,0:T(8,128)(2,1)}) custom-call(s32[4]{0:T(128)S(1)} %pad_add_fusion.3.pos_ref, s32[1,128]{1,0:T(1,128)S(1)} %get-tuple-element.136.tgt_ref, s32[1,128]{1,0:T(1,128)S(1)} %get-tuple-element.129.rank_ref, bf16[512,5120]{1,0:T(8,128)(2,1)} %own_hbm.3, ...), custom_call_target="tpu_custom_call" | custom-call | flops 2684354560 | bytes 14417920 | tf_op jit(solution)/shard_map/forward_a/pallas_call | solution.py:303
  50.6 1.5 %collective-permute-done.7.refs_2_ = bf16[16,5120]{1,0:T(8,128)(2,1)S(1)} collective-permute-done((bf16[16,5120]{1,0:T(8,128)(2,1)S(1)}, bf16[16,5120]{1,0:T(8,128)(2,1)S(1)}, u32[]{:S(2)}, u32[]{:S(2)}) %collective-permute-start.7) | collective-permute-done | bytes 163872 | tf_op jit(solution)/shard_map/ppermute | solution.py:327
  52.7 7.4 %all-to-all-start.5 = ((bf16[16,352,128]{2,1,0:T(8,128)(2,1)}), bf16[16,352,128]{2,1,0:T(8,128)(2,1)S(1)}, u32[]{:S(2)}, u32[]{:S(2)}) async-start(bf16[16,352,128]{2,1,0:T(8,128)(2,1)} %get-tuple-element.92), calls=%async_computation.5 | async-start | bytes 2883584 | tf_op jit(solution)/shard_map/all_to_all | solution.py:332
  61.9 10.2 %forward_b.1 = (f32[1024,128]{1,0:T(8,128)}, bf16[128,5120]{1,0:T(8,128)(2,1)}, bf16[16,352,128]{2,1,0:T(8,128)(2,1)}) custom-call(s32[4]{0:T(128)S(1)} %pad_add_fusion.3.pos_ref, s32[1,128]{1,0:T(1,128)S(1)} %get-tuple-element.137.tgt_ref, s32[1,128]{1,0:T(1,128)S(1)} %get-tuple-element.128.rank_ref, bf16[512,5120]{1,0:T(8,128)(2,1)} %own_hbm.3, ...), custom_call_target="tpu_custom_call" | custom-call | flops 2684354560 | bytes 14417920 | tf_op jit(solution)/shard_map/forward_b/pallas_call | solution.py:303
  72.1 5.6 %all-to-all-done.5.got_ref = bf16[16,352,128]{2,1,0:T(8,128)(2,1)S(1)} async-done(((bf16[16,352,128]{2,1,0:T(8,128)(2,1)}), bf16[16,352,128]{2,1,0:T(8,128)(2,1)S(1)}, u32[]{:S(2)}, u32[]{:S(2)}) %all-to-all-start.5) | async-done | bytes 1441824 | tf_op jit(solution)/shard_map/all_to_all | solution.py:332
  77.7 5.0 %all-to-all-start.6 = ((bf16[16,352,128]{2,1,0:T(8,128)(2,1)}), bf16[16,352,128]{2,1,0:T(8,128)(2,1)S(1)}, u32[]{:S(2)}, u32[]{:S(2)}) async-start(bf16[16,352,128]{2,1,0:T(8,128)(2,1)} %get-tuple-element.98), calls=%async_computation.6 | async-start | bytes 2883584 | tf_op jit(solution)/shard_map/all_to_all | solution.py:334
  85.0 15.9 %all-to-all-done.6.got_ref = bf16[16,352,128]{2,1,0:T(8,128)(2,1)S(1)} async-done(((bf16[16,352,128]{2,1,0:T(8,128)(2,1)}), bf16[16,352,128]{2,1,0:T(8,128)(2,1)S(1)}, u32[]{:S(2)}, u32[]{:S(2)}) %all-to-all-start.6) | async-done | bytes 1441824 | tf_op jit(solution)/shard_map/all_to_all | solution.py:334
  101.1 1.8 %combine.1 = bf16[8,40,640]{2,1,0:T(8,128)(2,1)} custom-call(s32[4]{0:T(128)S(1)} %pad_add_fusion.3.pos_ref, s32[1,128]{1,0:T(1,128)S(1)} %get-tuple-element.133.place_ref, f32[320,256]{1,0:T(8,128)S(1)} %get-tuple-element.138.more_ref, bf16[16,352,128]{2,1,0:T(8,128)(2,1)S(1)} %all-to-all-done.6.got_ref, bf16[128,640]{1,0:T(8,128)(2,1)S(1)} %get-tuple-element.101.first_ref, ...), custom_call_target="tpu_custom_call" | custom-call | flops 1000000 | bytes 100000 | tf_op jit(solution)/shard_map/combine/pallas_call | solution.py:353
  102.9 6.0 %all-to-all-start.7 = ((bf16[8,40,640]{2,1,0:T(8,128)(2,1)}), bf16[8,40,640]{2,1,0:T(8,128)(2,1)S(1)}, u32[]{:S(2)}, u32[]{:S(2)}) async-start(bf16[8,40,640]{2,1,0:T(8,128)(2,1)} %combine.1), calls=%async_computation.7 | async-start | bytes 819200 | tf_op jit(solution)/shard_map/all_to_all | solution.py:362
  109.7 11.3 %all-to-all-done.7.got = bf16[8,40,640]{2,1,0:T(8,128)(2,1)S(1)} async-done(((bf16[8,40,640]{2,1,0:T(8,128)(2,1)}), bf16[8,40,640]{2,1,0:T(8,128)(2,1)S(1)}, u32[]{:S(2)}, u32[]{:S(2)}) %all-to-all-start.7) | async-done | bytes 409632 | tf_op jit(solution)/shard_map/all_to_all | solution.py:362
  121.0 1.5 %finish.1 = (bf16[32,320]{1,0:T(8,128)(2,1)}, f32[8,256]{1,0:T(8,128)S(1)}) custom-call(s32[4]{0:T(128)S(1)} %pad_add_fusion.3.pos_ref, bf16[8,40,640]{2,1,0:T(8,128)(2,1)S(1)} %all-to-all-done.7.got), custom_call_target="tpu_custom_call" | custom-call | flops 1000000 | bytes 100000 | tf_op jit(solution)/shard_map/finish/pallas_call | solution.py:364
  122.6 1.1 collective-permute-done.9.stat_oth
  123.7 10.3 %grad_table.1 = (bf16[512,5120]{1,0:T(8,128)(2,1)}, f32[1,1]{1,0:T(1,128)}) custom-call(s32[4]{0:T(128)S(1)} %pad_add_fusion.3.pos_ref, s32[1,512]{1,0:T(1,128)S(1)} %reshape.190.tok_ref, s32[1,256]{1,0:T(1,128)S(1)} %get-tuple-element.123.tgt_own, s32[1,256]{1,0:T(1,128)S(1)} %get-tuple-element.127.tgt_oth, f32[8,256]{1,0:T(8,128)S(1)} %get-tuple-element.104.stat_own, ...), custom_call_target="tpu_custom_call" | custom-call | flops 5368709120 | bytes 15728640 | tf_op jit(solution)/shard_map/grad_table/pallas_call | solution.py:378
  (59 shorter events, 8.5 us)
Async XLA Ops:
  7.2 33.6 %collective-permute-start.8 = (bf16[512,5120]{1,0:T(8,128)(2,1)}, bf16[512,5120]{1,0:T(8,128)(2,1)}, u32[]{:S(2)}, u32[]{:S(2)}) collective-permute-start(bf16[512,5120]{1,0:T(8,128)(2,1)} %own_hbm.3), channel_id=1, source_target_pairs={{0,1},{1,0},{2,3},{3,2},{4,5},{5,4},{6,7},{7,6},{8,9},{9,8},{10,11... | collective-permute-start | bytes 15728648 | tf_op jit(solution)/shard_map/ppermute | solution.py:245
  7.3 14.4 %collective-permute-start = (bf16[32,5120]{1,0:T(8,128)(2,1)}, bf16[32,5120]{1,0:T(8,128)(2,1)S(1)}, u32[]{:S(2)}, u32[]{:S(2)}) collective-permute-start(bf16[32,5120]{1,0:T(8,128)(2,1)} %refs_1_.1), channel_id=1, source_target_pairs={{0,2},{2,4},{4,6},{6,8},{8,10},{10,12},{12,14},{14,0},{1,3},{3,5},... | collective-permute-start | bytes 983048 | tf_op jit(solution)/shard_map/ppermute | solution.py:249
  9.3 12.4 %collective-permute-start.1 = (bf16[32,5120]{1,0:T(8,128)(2,1)}, bf16[32,5120]{1,0:T(8,128)(2,1)S(1)}, u32[]{:S(2)}, u32[]{:S(2)}) collective-permute-start(bf16[32,5120]{1,0:T(8,128)(2,1)} %refs_1_.1), channel_id=1, source_target_pairs={{0,14},{2,0},{4,2},{6,4},{8,6},{10,8},{12,10},{14,12},{1,15},{3,1}... | collective-permute-start | bytes 983048 | tf_op jit(solution)/shard_map/ppermute | solution.py:249
  14.6 13.4 %all-to-all-start.4 = ((s32[16,1,64]{2,1,0:T(1,128)}), s32[16,1,64]{2,1,0:T(1,128)S(1)}, u32[]{:S(2)}, u32[]{:S(2)}) async-start(s32[16,1,64]{2,1,0:T(1,128)} %broadcast_in_dim.13), calls=%async_computation.4 | async-start | bytes 16384 | tf_op jit(solution)/shard_map/all_to_all | solution.py:247
  20.5 103.2 %all-gather.2.cloned.1.call-start = ((), (), s32[]{:S(2)}) async-start(), calls=%async_computation.8 | async-start | bytes 5570560 | tf_op jit(solution)/shard_map/all_gather | solution.py:337
  21.7 10.8 %collective-permute-start.2 = (bf16[32,5120]{1,0:T(8,128)(2,1)S(1)}, bf16[32,5120]{1,0:T(8,128)(2,1)S(1)}, u32[]{:S(2)}, u32[]{:S(2)}) collective-permute-start(bf16[32,5120]{1,0:T(8,128)(2,1)S(1)} %collective-permute-done.refs_0_), channel_id=1, source_target_pairs={{0,2},{2,4},{4,6},{6,8},{8,10},{10,12},{12,14},{14,0},{1,3},{3,5},... | collective-permute-start | bytes 983048 | tf_op jit(solution)/shard_map/ppermute | solution.py:251
  22.6 9.9 %collective-permute-start.3 = (bf16[32,5120]{1,0:T(8,128)(2,1)S(1)}, bf16[32,5120]{1,0:T(8,128)(2,1)S(1)}, u32[]{:S(2)}, u32[]{:S(2)}) collective-permute-start(bf16[32,5120]{1,0:T(8,128)(2,1)S(1)} %collective-permute-done.1.refs_2_), channel_id=1, source_target_pairs={{0,14},{2,0},{4,2},{6,4},{8,6},{10,8},{12,10},{14,12},{1,15},{3,1}... | collective-permute-start | bytes 983048 | tf_op jit(solution)/shard_map/ppermute | solution.py:251
  32.5 19.6 %collective-permute-start.4 = (bf16[32,5120]{1,0:T(8,128)(2,1)S(1)}, bf16[32,5120]{1,0:T(8,128)(2,1)S(1)}, u32[]{:S(2)}, u32[]{:S(2)}) collective-permute-start(bf16[32,5120]{1,0:T(8,128)(2,1)S(1)} %collective-permute-done.2.refs_4_), channel_id=1, source_target_pairs={{0,2},{2,4},{4,6},{6,8},{8,10},{10,12},{12,14},{14,0},{1,3},{3,5},... | collective-permute-start | bytes 983048 | tf_op jit(solution)/shard_map/ppermute | solution.py:329
  34.4 17.7 %collective-permute-start.5 = (bf16[32,5120]{1,0:T(8,128)(2,1)S(1)}, bf16[32,5120]{1,0:T(8,128)(2,1)S(1)}, u32[]{:S(2)}, u32[]{:S(2)}) collective-permute-start(bf16[32,5120]{1,0:T(8,128)(2,1)S(1)} %collective-permute-done.3.refs_3_), channel_id=1, source_target_pairs={{0,14},{2,0},{4,2},{6,4},{8,6},{10,8},{12,10},{14,12},{1,15},{3,1}... | collective-permute-start | bytes 983048 | tf_op jit(solution)/shard_map/ppermute | solution.py:329
  36.2 14.4 %collective-permute-start.6 = (bf16[16,5120]{1,0:T(8,128)(2,1)S(1)}, bf16[16,5120]{1,0:T(8,128)(2,1)S(1)}, u32[]{:S(2)}, u32[]{:S(2)}) collective-permute-start(bf16[16,5120]{1,0:T(8,128)(2,1)S(1)} %slice.39), channel_id=1, source_target_pairs={{0,4},{2,6},{4,8},{6,10},{8,12},{10,14},{12,0},{14,2},{1,5},{3,7},... | collective-permute-start | bytes 491528 | tf_op jit(solution)/shard_map/ppermute | solution.py:326
  38.9 13.1 %collective-permute-start.7 = (bf16[16,5120]{1,0:T(8,128)(2,1)S(1)}, bf16[16,5120]{1,0:T(8,128)(2,1)S(1)}, u32[]{:S(2)}, u32[]{:S(2)}) collective-permute-start(bf16[16,5120]{1,0:T(8,128)(2,1)S(1)} %slice.40), channel_id=1, source_target_pairs={{0,12},{2,14},{4,0},{6,2},{8,4},{10,6},{12,8},{14,10},{1,13},{3,15... | collective-permute-start | bytes 491528 | tf_op jit(solution)/shard_map/ppermute | solution.py:327
  50.6 1.5 %copy-start = (bf16[16,5120]{1,0:T(8,128)(2,1)}, bf16[16,5120]{1,0:T(8,128)(2,1)S(1)}, u32[]{:S(2)}) copy-start(bf16[16,5120]{1,0:T(8,128)(2,1)S(1)} %collective-permute-done.6.refs_1_) | copy-start | bytes 491524
  52.7 25.0 %all-to-all-start.5 = ((bf16[16,352,128]{2,1,0:T(8,128)(2,1)}), bf16[16,352,128]{2,1,0:T(8,128)(2,1)S(1)}, u32[]{:S(2)}, u32[]{:S(2)}) async-start(bf16[16,352,128]{2,1,0:T(8,128)(2,1)} %get-tuple-element.92), calls=%async_computation.5 | async-start | bytes 2883584 | tf_op jit(solution)/shard_map/all_to_all | solution.py:332
  60.1 0.9 copy-start.1
  61.0 0.9 copy-start.3
  77.7 23.2 %all-to-all-start.6 = ((bf16[16,352,128]{2,1,0:T(8,128)(2,1)}), bf16[16,352,128]{2,1,0:T(8,128)(2,1)S(1)}, u32[]{:S(2)}, u32[]{:S(2)}) async-start(bf16[16,352,128]{2,1,0:T(8,128)(2,1)} %get-tuple-element.98), calls=%async_computation.6 | async-start | bytes 2883584 | tf_op jit(solution)/shard_map/all_to_all | solution.py:334
  82.7 39.9 %collective-permute-start.12 = (bf16[128,5120]{1,0:T(8,128)(2,1)}, bf16[128,5120]{1,0:T(8,128)(2,1)}, u32[]{:S(2)}, u32[]{:S(2)}) collective-permute-start(bf16[128,5120]{1,0:T(8,128)(2,1)} %get-tuple-element.107.refs_4_), channel_id=1, source_target_pairs={{0,1},{1,0},{2,3},{3,2},{4,5},{5,4},{6,7},{7,6},{8,9},{9,8},{10,11... | collective-permute-start | bytes 3932168 | tf_op jit(solution)/shard_map/ppermute | solution.py:340
  82.7 39.9 %collective-permute-start.13 = (bf16[128,5120]{1,0:T(8,128)(2,1)}, bf16[128,5120]{1,0:T(8,128)(2,1)}, u32[]{:S(2)}, u32[]{:S(2)}) collective-permute-start(bf16[128,5120]{1,0:T(8,128)(2,1)} %get-tuple-element.108.refs_5_), channel_id=1, source_target_pairs={{0,1},{1,0},{2,3},{3,2},{4,5},{5,4},{6,7},{7,6},{8,9},{9,8},{10,11... | collective-permute-start | bytes 3932168 | tf_op jit(solution)/shard_map/ppermute | solution.py:340
  101.1 7.9 %copy-start.4 = (f32[1024,128]{1,0:T(8,128)S(1)}, f32[1024,128]{1,0:T(8,128)}, u32[]{:S(2)}) copy-start(f32[1024,128]{1,0:T(8,128)} %get-tuple-element.105.refs_0_) | copy-start | bytes 1572868
  101.1 8.0 %copy-start.5 = (f32[1024,128]{1,0:T(8,128)S(1)}, f32[1024,128]{1,0:T(8,128)}, u32[]{:S(2)}) copy-start(f32[1024,128]{1,0:T(8,128)} %get-tuple-element.106.refs_1_) | copy-start | bytes 1572868
  102.9 18.1 %all-to-all-start.7 = ((bf16[8,40,640]{2,1,0:T(8,128)(2,1)}), bf16[8,40,640]{2,1,0:T(8,128)(2,1)S(1)}, u32[]{:S(2)}, u32[]{:S(2)}) async-start(bf16[8,40,640]{2,1,0:T(8,128)(2,1)} %combine.1), calls=%async_computation.7 | async-start | bytes 819200 | tf_op jit(solution)/shard_map/all_to_all | solution.py:362
  109.0 13.6 %collective-permute-start.10 = (f32[512,128]{1,0:T(8,128)S(1)}, f32[512,128]{1,0:T(8,128)S(1)}, u32[]{:S(2)}, u32[]{:S(2)}) collective-permute-start(f32[512,128]{1,0:T(8,128)S(1)} %slice.46), channel_id=1, source_target_pairs={{0,1},{1,0},{2,3},{3,2},{4,5},{5,4},{6,7},{7,6},{8,9},{9,8},{10,11... | collective-permute-start | bytes 786440 | tf_op jit(solution)/shard_map/ppermute | solution.py:340
  109.1 13.4 %collective-permute-start.11 = (f32[512,128]{1,0:T(8,128)S(1)}, f32[512,128]{1,0:T(8,128)S(1)}, u32[]{:S(2)}, u32[]{:S(2)}) collective-permute-start(f32[512,128]{1,0:T(8,128)S(1)} %slice.47), channel_id=1, source_target_pairs={{0,1},{1,0},{2,3},{3,2},{4,5},{5,4},{6,7},{7,6},{8,9},{9,8},{10,11... | collective-permute-start | bytes 786440 | tf_op jit(solution)/shard_map/ppermute | solution.py:340
  122.5 1.2 collective-permute-start.9
  (1 other events, 0.7 us)
Sparse Core Ops, SparseCore 0:
  52.2 42.5 all-gather.1
